TPU v7x, 32 devices: a whole 2x2x4 slice. The times are simulated.
32 devices in a mesh: seq: 16 (over z, y, x), mp: 2 (over core).
Axes of the slice: x: 2, y: 2, z: 4, core: 2. Of those that a mesh axis runs over, the one named last changes fastest.
Arguments:
- patch_states: bfloat16 [8192, 2048], P('seq'), may hold values from -6 to 6
- mlp_gain: bfloat16 [2048], replicated, may hold values from 0.099609375 to 1.8984375
- up_weight: bfloat16 [2048, 7168], P('seq', 'mp')
- down_weight: bfloat16 [7168, 2048], P('mp', 'seq')
- kv_gain: bfloat16 [2048], replicated, may hold values from 0.099609375 to 1.8984375
- kv_weight: bfloat16 [2048, 2048], P(None, 'mp'), may hold values from -0.125 to 0.125
- byte_states: bfloat16 [16384, 1024], P('seq'), may hold values from -6 to 6
- query_weight: bfloat16 [1024, 1024], P(None, 'mp'), may hold values from -0.1875 to 0.1875
- out_weight: bfloat16 [1024, 1024], P('mp'), may hold values from -0.75 to 0.75
- patch_counts: int32 [16], P('seq'), may hold values from 256 to 512, as said below
- byte_patch: int32 [16384], P('seq'), may hold values from 0 to 511, as said below
Outputs:
- decoded: bfloat16 [16384, 1024], P(('seq', 'mp'))
Inputs may be any that keep to these rules, and one draw needn't show every extreme that they name: `patch_counts`: exactly 512 in some block and exactly 256 in another, in every draw. `byte_patch`: within each seq block of 1024 bytes the values start at 0, never fall, rise by at most one from one byte to the next, and end at that block's patch count minus one.
All inputs are finite; a program needn't handle non-finite values.
Results may differ from a plain program's by a relative error of at most 0.02.
Values may be sent and summed in bfloat16 or wider, within the bound.
A program may use at most 128 MiB of HBM per device.

v0:
```python
import math

import jax
import jax.numpy as jnp
from jax import lax
from jax.sharding import PartitionSpec as P

HS = 128
WIN = 1024


def entering(value, axis, join, neutral):
    count, mine = (lax.axis_size(axis), lax.axis_index(axis))
    pieces = jax.tree.map(lambda part: lax.all_gather(part, axis), value)
    so_far = jax.tree.map(
        lambda part, zero: jnp.full_like(part, 0) + jnp.asarray(zero, part.dtype), value, neutral
    )

    def step(position, so_far):
        longer = join(so_far, jax.tree.map(lambda part: part[position], pieces))
        return jax.tree.map(lambda new, old: jnp.where(position < mine, new, old), longer, so_far)

    return lax.fori_loop(0, count - 1, step, so_far)


def from_behind(value, axis, steps):
    count = lax.axis_size(axis)
    leading, last = (max(0, -steps), min(count, count - steps))
    return lax.ppermute(value, axis, [(source, source + steps) for source in range(leading, last)])


def scale_rows(values, gain):
    return values * lax.rsqrt(jnp.mean(values * values, axis=-1, keepdims=True) + 1e-05) * gain


def unit_rows(values):
    return values * lax.rsqrt(jnp.mean(values * values, axis=-1, keepdims=True) + 1e-06)


def on_device(
    patch_states,
    mlp_gain,
    up_weight,
    down_weight,
    kv_gain,
    kv_weight,
    byte_states,
    query_weight,
    out_weight,
    patch_counts,
    byte_patch,
):
    patch_rows = patch_states.shape[0]
    normed = scale_rows(patch_states.astype(jnp.float32), mlp_gain.astype(jnp.float32)).astype(
        jnp.bfloat16
    )
    preact = jnp.dot(
        normed,
        lax.all_gather(up_weight, "seq", axis=0, tiled=True),
        preferred_element_type=jnp.float32,
    )
    hidden = jax.nn.gelu(preact, approximate=False).astype(jnp.bfloat16)
    kv_scale = kv_gain.astype(jnp.float32)
    partial_value = jnp.dot(
        hidden,
        lax.all_gather(down_weight, "seq", axis=1, tiled=True),
        preferred_element_type=jnp.float32,
    )
    mixed_out = lax.psum(partial_value.astype(jnp.bfloat16), "mp").astype(jnp.float32)
    kv_in = scale_rows(patch_states.astype(jnp.float32) + mixed_out, kv_scale).astype(jnp.bfloat16)
    heads_here = kv_weight.shape[1] // (2 * HS)
    projected = jnp.dot(kv_in, kv_weight, preferred_element_type=jnp.float32).reshape(
        patch_rows, heads_here, 2, HS
    )
    keys = unit_rows(projected[:, :, 0])
    kv_pack = (
        jnp.stack([keys, projected[:, :, 1]], axis=2)
        .astype(jnp.bfloat16)
        .reshape(patch_rows, heads_here * 2 * HS)
    )
    bytes_here = byte_states.shape[0]
    query_proj = jnp.dot(byte_states, query_weight, preferred_element_type=jnp.float32).reshape(
        bytes_here, heads_here, HS
    )
    queries = unit_rows(query_proj).astype(jnp.bfloat16)
    depth_back = (WIN + patch_rows // 2 - 2) // (patch_rows // 2)
    own_count = patch_counts[0]
    slots = jnp.arange(depth_back, dtype=jnp.int32)

    def join_windows(earlier_part, later_part):
        early_vals, early_len = earlier_part
        late_vals, late_len = later_part
        from_late = slots >= depth_back - late_len
        wanted = slots + late_len
        early_pick = jnp.sum(
            jnp.where(slots[None, :] == wanted[:, None], early_vals[None, :], 0), axis=1
        ).astype(jnp.int32)
        joined = jnp.where(from_late, late_vals, early_pick).astype(jnp.int32)
        return (joined, jnp.minimum(early_len + late_len, depth_back).astype(jnp.int32))

    own_window = jnp.where(slots == depth_back - 1, own_count, 0)
    empty_window = (jnp.zeros((depth_back,), jnp.int32), jnp.zeros((), jnp.int32))
    prior_counts, prior_len = entering(
        (own_window, jnp.ones((), jnp.int32)), "seq", join_windows, empty_window
    )
    earlier = []
    for offset_back in range(1, depth_back + 1):
        earlier.append(from_behind(kv_pack, "seq", offset_back))
    score_scale = 2.0 / math.sqrt(HS)
    positions = jnp.arange(patch_rows, dtype=jnp.int32)
    numerator = jnp.zeros((bytes_here, heads_here, HS), jnp.float32)
    denominator = jnp.zeros((heads_here, bytes_here), jnp.float32)
    for distance, kv_block in enumerate([kv_pack] + earlier):
        if distance == 0:
            first_id = jnp.zeros((), jnp.int32)
            live_count = own_count
        else:
            first_id = -jnp.sum(prior_counts[depth_back - distance :]).astype(jnp.int32)
            live_count = prior_counts[depth_back - distance]
        key_ids = first_id + positions
        usable = (
            (positions < live_count)[None, :]
            & (key_ids[None, :] <= byte_patch[:, None])
            & (key_ids[None, :] > byte_patch[:, None] - WIN)
        )
        kv_parts = kv_block.reshape(patch_rows, heads_here, 2, HS)
        scores = (
            jnp.einsum(
                "bhd,phd->hbp", queries, kv_parts[:, :, 0], preferred_element_type=jnp.float32
            )
            * score_scale
        )
        weights = jnp.where(usable[None], jnp.exp(scores), 0.0)
        numerator = numerator + jnp.einsum(
            "hbp,phd->bhd",
            weights.astype(jnp.bfloat16),
            kv_parts[:, :, 1],
            preferred_element_type=jnp.float32,
        )
        denominator = denominator + jnp.sum(weights, axis=-1)
    attended = (
        (numerator / jnp.transpose(denominator)[:, :, None])
        .astype(jnp.bfloat16)
        .reshape(bytes_here, heads_here * HS)
    )
    decoded = lax.psum_scatter(
        jnp.dot(attended, out_weight, preferred_element_type=jnp.float32).astype(jnp.bfloat16),
        "mp",
        scatter_dimension=0,
        tiled=True,
    )
    return decoded


def solution(mesh):
    in_specs = (
        P("seq", None),
        P(),
        P("seq", "mp"),
        P("mp", "seq"),
        P(),
        P(None, "mp"),
        P("seq", None),
        P(None, "mp"),
        P("mp", None),
        P("seq"),
        P("seq"),
    )
    out_specs = P(("seq", "mp"), None)
    return jax.shard_map(
        on_device, mesh=mesh, in_specs=in_specs, out_specs=out_specs, check_vma=False
    )
```

profile of v0, /device:TPU:9, one launch (start us, length us, event | category | flops | bytes accessed | tf_op | source)
XLA Modules:
  0.0 619.3 jit_solution(12647247137764621798)
XLA Ops:
  6.5 0.7 all-gather.4.cloned.1.call-update
  7.3 0.7 all-gather.6.cloned.1.call-update
  8.7 0.7 convert_element_type.57
  9.4 1.3 dynamic-slice
  10.7 0.7 dynamic-update-slice
  11.4 9.8 %all-reduce = s32[16]{0:T(128)S(1)} all-reduce(s32[16]{0:T(128)S(1)} %dynamic-update-slice), channel_id=1, replica_groups=mesh['seq'=16,'mp'=2] {'seq'}, use_global_device_ids=true, to_apply=%add | all-reduce | flops 16 | bytes 128
  21.3 25.7 %all-gather = s32[16,1,4]{2,1,0:T(1,128)S(1)} all-gather(s32[1,1,4]{2,1,0:T(1,128)S(1)} %fusion.108), channel_id=1, replica_groups=mesh['seq'=16,'mp'=2] {'seq'}, dimensions={0}, use_global_device_ids=true | all-gather | bytes 272 | tf_op jit(solution)/shard_map/all_gather | solution.py:14
  46.9 31.0 %while.15 = (s32[]{:T(128)}, s32[4]{0:T(128)S(1)}, s32[]{:T(128)}, s32[16]{0:T(128)S(1)}, s32[16,4]{1,0:T(8,128)S(1)}, /*index=5*/s32[]{:T(128)}, s32[]{:T(128)}, s32[]{:T(128)}) while((s32[]{:T(128)}, s32[4]{0:T(128)S(1)}, s32[]{:T(128)}, s32[16]{0:T(128)S(1)}, s32[16,4]{1,0:T(8,128)S(1)}, /*index=5*/s32[]{:T(128)}, ...), condition=%wide.region_7.8_spmd.clone.clone, body=%wide.region_5.7_spmd.clone.clone.sunk | while | flops 69 | bytes 309 | solution.py:23
  46.9 0.6 dynamic_slice.22
  48.2 0.6 broadcast_select_fusion.4
  49.0 0.6 dynamic_slice.22
  51.1 0.6 dynamic_slice.22
  52.3 0.6 broadcast_select_fusion.4
  53.1 0.6 dynamic_slice.22
  54.4 0.6 broadcast_select_fusion.4
  55.2 0.6 dynamic_slice.22
  57.3 0.6 dynamic_slice.22
  59.4 0.6 dynamic_slice.22
  61.4 0.6 dynamic_slice.22
  63.5 0.6 dynamic_slice.22
  65.6 0.6 dynamic_slice.22
  67.6 0.6 dynamic_slice.22
  69.7 0.6 dynamic_slice.22
  71.8 0.6 dynamic_slice.22
  73.8 0.6 dynamic_slice.22
  75.9 0.6 dynamic_slice.22
  78.0 0.7 slice_reduce_fusion
  78.7 0.7 fusion.149
  79.4 2.1 fusion.22
  81.4 3.8 multiply_reduce_fusion.1
  85.3 95.8 %all-gather.4.cloned.1.call-done = bf16[2048,3584]{1,0:T(8,128)(2,1)} async-done(((bf16[128,3584]{1,0:T(8,128)(2,1)}), bf16[2048,3584]{1,0:T(8,128)(2,1)}) %all-gather.4.cloned.1.call-update) | async-done | bytes 14680080 | tf_op jit(solution)/shard_map/all_gather | solution.py:59
  181.1 223.7 %all-gather.6.cloned.1.call-done = bf16[3584,2048]{1,0:T(8,128)(2,1)} async-done(((bf16[3584,128]{1,0:T(8,128)(2,1)}), bf16[3584,2048]{1,0:T(8,128)(2,1)}) %all-gather.6.cloned.1.call-update) | async-done | bytes 14680080 | tf_op jit(solution)/shard_map/all_gather | solution.py:66
  404.8 37.9 %fusion.82 = bf16[512,2048]{1,0:T(8,128)(2,1)} fusion(bf16[3584,2048]{1,0:T(8,128)(2,1)} %all-gather.6.cloned.1.call-done, bf16[2048,3584]{1,0:T(8,128)(2,1)} %all-gather.4.cloned.1.call-done, bf16[512,2048]{1,0:T(8,128)(2,1)} %param.13, f32[2048]{0:T(1024)S(1)} %convert_element_type.57, f32[512]{0:T(512)S(1)} %add_rsqrt_fusion.3), kind=kOutput, calls=%fused_computation.100 | convolution fusion | flops 15156903936 | bytes 33564672 | tf_op jit(solution)/shard_map/dot_general | solution.py:64
  442.9 0.7 slice_reduce_fusion.1
  443.6 0.6 reduce_sum.131
  446.7 2.9 copy.69
  449.6 1.2 iota_compare_fusion.5
  450.8 1.3 iota_compare_fusion.3
  452.1 2.8 multiply_convert_fusion.2
  455.0 3.7 compare_and_fusion
  458.7 6.6 %all-reduce.3.cloned.1.call-done = bf16[512,2048]{1,0:T(8,128)(2,1)} async-done(((bf16[512,2048]{1,0:T(8,128)(2,1)}), bf16[512,2048]{1,0:T(8,128)(2,1)}) %all-reduce.3.cloned.1.call-update) | async-done | bytes 2097168 | tf_op jit(solution)/shard_map/psum | solution.py:69
  465.3 2.3 multiply_reduce_fusion
  467.7 6.5 %fusion.85 = f32[512,1024]{1,0:T(8,128)} fusion(bf16[2048,1024]{1,0:T(8,128)(2,1)} %param.18, bf16[512,2048]{1,0:T(8,128)(2,1)} %all-reduce.3.cloned.1.call-done, bf16[512,2048]{1,0:T(8,128)(2,1)S(1)} %copy-done.2, f32[2048]{0:T(1024)S(1)} %convert_element_type.62, f32[512]{0:T(512)S(1)} %add_rsqrt_fusion.2), kind=kOutput, calls=%fused_computation.101 | convolution fusion | flops 2153775104 | bytes 10496000 | tf_op jit(solution)/shard_map/dot_general | solution.py:72
  474.2 4.0 reshape.423
  478.3 2.3 slice.73
  480.6 2.7 slice.74
  484.2 1.3 copy.72
  485.5 3.1 collective-permute-start.3
  488.6 4.0 collective-permute-start.2
  492.6 3.1 collective-permute-start.1
  495.7 2.2 collective-permute-start
  498.0 3.6 fusion.12
  501.6 1.8 fusion.33
  503.4 78.0 %collective-permute-done = bf16[512,1024]{0,1:T(8,128)(2,1)S(1)} collective-permute-done((bf16[512,1024]{0,1:T(8,128)(2,1)}, bf16[512,1024]{0,1:T(8,128)(2,1)S(1)}, u32[]{:S(2)}, u32[]{:S(2)}) %collective-permute-start) | collective-permute-done | bytes 1048608 | tf_op jit(solution)/shard_map/ppermute | solution.py:29
  581.4 2.8 fusion.14
  584.2 1.8 fusion.31
  586.0 2.6 fusion.16
  588.6 1.8 fusion.29
  590.4 2.6 fusion.18
  592.9 1.8 fusion.27
  594.7 2.6 fusion.20
  597.4 2.2 fusion.92
  599.7 2.6 convolution_convert_fusion
  602.4 9.9 %reduce-scatter.2.cloned.1.call-done = bf16[512,1024]{1,0:T(8,128)(2,1)} async-done(((bf16[1024,1024]{1,0:T(8,128)(2,1)}), bf16[512,1024]{1,0:T(8,128)(2,1)}) %reduce-scatter.2.cloned.1.call-update) | async-done | bytes 1048592 | tf_op jit(solution)/shard_map/reduce_scatter | solution.py:146
  (88 shorter events, 11.4 us)
Async XLA Ops:
  6.5 74.9 %copy-start = (bf16[1024,1024]{1,0:T(8,128)(2,1)S(1)}, bf16[1024,1024]{1,0:T(8,128)(2,1)}, u32[]{:S(2)}) copy-start(bf16[1024,1024]{1,0:T(8,128)(2,1)} %param.19) | copy-start | bytes 6291460
  6.5 174.6 %all-gather.4.cloned.1.call-start = ((), (), s32[]{:S(2)}) async-start(), calls=%async_computation.1 | async-start | bytes 15597568 | tf_op jit(solution)/shard_map/all_gather | solution.py:59
  7.3 397.6 %all-gather.6.cloned.1.call-start = ((), (), s32[]{:S(2)}) async-start(), calls=%async_computation.2 | async-start | bytes 15597568 | tf_op jit(solution)/shard_map/all_gather | solution.py:66
  8.0 457.3 %all-reduce.3.cloned.1.call-start = ((), (), s32[]{:S(2)}) async-start(), calls=%async_computation.3 | async-start | bytes 4194304 | tf_op jit(solution)/shard_map/psum | solution.py:69
  85.3 361.4 %copy-start.8 = (bf16[2048]{0:T(1024)(128)(2,1)S(1)}, bf16[2048]{0:T(1024)(128)(2,1)}, u32[]{:S(2)}) copy-start(bf16[2048]{0:T(1024)(128)(2,1)} %param.17) | copy-start | bytes 12292
  85.3 366.8 %copy-start.7 = (s32[1024]{0:T(1024)S(1)}, s32[1024]{0:T(1024)}, u32[]{:S(2)}) copy-start(s32[1024]{0:T(1024)} %param.23) | copy-start | bytes 12292
  442.8 22.6 %copy-start.2 = (bf16[512,2048]{1,0:T(8,128)(2,1)S(1)}, bf16[512,2048]{1,0:T(8,128)(2,1)}, u32[]{:S(2)}) copy-start(bf16[512,2048]{1,0:T(8,128)(2,1)} %param.13) | copy-start | bytes 6291460
  442.8 169.5 %reduce-scatter.2.cloned.1.call-start = ((), (), s32[]{:S(2)}) async-start(), calls=%async_computation.4 | async-start | bytes 3145728 | tf_op jit(solution)/shard_map/reduce_scatter | solution.py:146
  484.2 17.4 %copy-start.4 = (pred[1024,512]{0,1:T(8,128)(4,1)S(1)}, pred[1024,512]{0,1:T(8,128)(4,1)}, u32[]{:S(2)}) copy-start(pred[1024,512]{0,1:T(8,128)(4,1)} %get-tuple-element.194) | copy-start | bytes 1572868
  485.5 109.2 %collective-permute-start.3 = (bf16[512,1024]{0,1:T(8,128)(2,1)}, bf16[512,1024]{0,1:T(8,128)(2,1)S(1)}, u32[]{:S(2)}, u32[]{:S(2)}) collective-permute-start(bf16[512,1024]{0,1:T(8,128)(2,1)} %bitcast.99), channel_id=1, source_target_pairs={{0,8},{2,10},{4,12},{6,14},{8,16},{10,18},{12,20},{14,22},{16,24},... | collective-permute-start | bytes 3145736 | tf_op jit(solution)/shard_map/ppermute | solution.py:29
  488.6 101.7 %collective-permute-start.2 = (bf16[512,1024]{0,1:T(8,128)(2,1)}, bf16[512,1024]{0,1:T(8,128)(2,1)S(1)}, u32[]{:S(2)}, u32[]{:S(2)}) collective-permute-start(bf16[512,1024]{0,1:T(8,128)(2,1)} %bitcast.100), channel_id=1, source_target_pairs={{0,6},{2,8},{4,10},{6,12},{8,14},{10,16},{12,18},{14,20},{16,22},{... | collective-permute-start | bytes 3145736 | tf_op jit(solution)/shard_map/ppermute | solution.py:29
  492.6 93.4 %collective-permute-start.1 = (bf16[512,1024]{0,1:T(8,128)(2,1)}, bf16[512,1024]{0,1:T(8,128)(2,1)S(1)}, u32[]{:S(2)}, u32[]{:S(2)}) collective-permute-start(bf16[512,1024]{0,1:T(8,128)(2,1)} %bitcast.101), channel_id=1, source_target_pairs={{0,4},{2,6},{4,8},{6,10},{8,12},{10,14},{12,16},{14,18},{16,20},{1... | collective-permute-start | bytes 3145736 | tf_op jit(solution)/shard_map/ppermute | solution.py:29
  495.7 85.7 %collective-permute-start = (bf16[512,1024]{0,1:T(8,128)(2,1)}, bf16[512,1024]{0,1:T(8,128)(2,1)S(1)}, u32[]{:S(2)}, u32[]{:S(2)}) collective-permute-start(bf16[512,1024]{0,1:T(8,128)(2,1)} %bitcast.102), channel_id=1, source_target_pairs={{0,2},{2,4},{4,6},{6,8},{8,10},{10,12},{12,14},{14,16},{16,18},{18... | collective-permute-start | bytes 3145736 | tf_op jit(solution)/shard_map/ppermute | solution.py:29
  501.6 79.8 %copy-start.3 = (pred[1024,512]{0,1:T(8,128)(4,1)S(1)}, pred[1024,512]{0,1:T(8,128)(4,1)}, u32[]{:S(2)}) copy-start(pred[1024,512]{0,1:T(8,128)(4,1)} %get-tuple-element.191) | copy-start | bytes 1572868
  501.6 79.8 %copy-start.5 = (bf16[1024,4,128]{2,0,1:T(8,128)(2,1)S(1)}, bf16[1024,4,128]{2,0,1:T(8,128)(2,1)}, u32[]{:S(2)}) copy-start(bf16[1024,4,128]{2,0,1:T(8,128)(2,1)} %multiply_convert_fusion.2) | copy-start | bytes 3145732
  592.9 1.8 copy-start.6
  597.4 2.3 copy-start.9
  597.4 14.9 %copy-start.1 = (bf16[1024,1024]{1,0:T(8,128)(2,1)S(1)}, bf16[1024,1024]{1,0:T(8,128)(2,1)}, u32[]{:S(2)}) copy-start(bf16[1024,1024]{1,0:T(8,128)(2,1)} %param.19) | copy-start | bytes 6291460
Sparse Core Ops, SparseCore 0:
  10.1 170.9 all-gather.3
  183.8 220.9 all-gather.5
  442.9 22.3 all-reduce.2
  602.5 9.7 reduce-scatter.1
where the time goes:
time: 624 us; the launch traced here: 619 us
  waiting for transfers between devices  416 us (67%)
  matrix products  74.5 us (12%)
  blocking collectives  35.5 us (6%)
  other arithmetic  29.2 us (5%)
  local copies, waits for them, and re-layouts  25.3 us (4%)
  between operations  17.1 us (3%)
  starting transfers between devices  12.5 us (2%)
  loops' own time  9.68 us (2%)
    all_gather x1, waiting for transfers between devices, on_device(): lax.all_gather(down_weight, 'seq', axis=1, tiled=True)  224 us
    all_gather x1, waiting for transfers between devices, on_device(): lax.all_gather(up_weight, 'seq', axis=0, tiled=True)  95.8 us
    ppermute x4, waiting for transfers between devices, from_behind(): lax.ppermute(value, axis, [(source, source + steps) for source in range(l...  78 us
    dot_general x1, matrix products, on_device(): jnp.dot(hidden, lax.all_gather(down_weight, 'seq', axis=1, tiled=True), p...  37.9 us
    all_gather x1, blocking collectives, entering(): pieces = jax.tree.map(lambda part: lax.all_gather(part, axis), value)  25.7 us
    dot_general x5, matrix products, on_device(): jnp.einsum('bhd,phd->hbp', queries, kv_parts[:, :, 0], preferred_element_...  14.2 us
  transfers between devices with their start and end apart: 8, of which 5 were waited for; matrix products, arithmetic and copies ran while one was open for 10% of the time, Pallas kernels for 0%

commit v1 on v0

v1 whole, which is shorter than its diff:
```python
import functools
import math

import jax
import jax.numpy as jnp
from jax import lax
from jax.experimental import pallas as pl
from jax.experimental.pallas import tpu as pltpu
from jax.sharding import PartitionSpec as P

HS = 128
WIN = 1024
KEY_TILE = 256


def scale_rows(values, gain):
    return values * lax.rsqrt(jnp.mean(values * values, axis=-1, keepdims=True) + 1e-05) * gain


def unit_rows(values):
    return values * lax.rsqrt(jnp.mean(values * values, axis=-1, keepdims=True) + 1e-06)


def sum_over_cores(value, scatter_dim):
    count = lax.axis_size("mp")
    if count != 2:
        return lax.psum_scatter(value, "mp", scatter_dimension=scatter_dim, tiled=True).astype(
            jnp.float32
        )
    me = lax.axis_index("mp")
    width = value.shape[scatter_dim] // 2
    theirs = lax.dynamic_slice_in_dim(value, (1 - me) * width, width, scatter_dim)
    mine = lax.dynamic_slice_in_dim(value, me * width, width, scatter_dim)
    got = lax.ppermute(theirs, "mp", [(0, 1), (1, 0)])
    return mine.astype(jnp.float32) + got.astype(jnp.float32)


def join_cores(value, dim):
    count = lax.axis_size("mp")
    if count != 2:
        return lax.all_gather(value, "mp", axis=dim, tiled=True)
    me = lax.axis_index("mp")
    got = lax.ppermute(value, "mp", [(0, 1), (1, 0)])
    first = jnp.where(me == 0, value, got)
    second = jnp.where(me == 0, got, value)
    return jnp.concatenate([first, second], axis=dim)


def attend_kernel(heads, distances, start, finish, scalars, ends, query, byte_patch, *refs):
    kv_refs, refs = refs[: len(distances)], refs[len(distances) :]
    if not start:
        (num_in, den_in), refs = refs[:2], refs[2:]
    if finish:
        out_weight, out, num, den = refs
    else:
        num, den = refs
    if start:
        num[...] = jnp.zeros_like(num)
        den[...] = jnp.zeros_like(den)
    else:
        num[...] = num_in[...]
        den[...] = den_in[...]
    tile = pl.program_id(0)
    lowest, highest = ends[2 * tile], ends[2 * tile + 1]
    scale = 2.0 / math.sqrt(HS) * math.log2(math.e)
    for distance, kv_ref in zip(distances, kv_refs):
        first, live = scalars[2 * distance], scalars[2 * distance + 1]
        for low in range(0, kv_ref.shape[0], KEY_TILE):
            last = first + jnp.minimum(live, low + KEY_TILE) - 1
            seen = (low < live) & (first + low <= highest) & (last > lowest - WIN)

            @pl.when(seen)
            def _(kv_ref=kv_ref, low=low, first=first, live=live):
                rows = query.shape[0]
                position = low + lax.broadcasted_iota(jnp.int32, (rows, KEY_TILE), 1)
                gap = byte_patch[...] - first - position
                usable = (position < live) & (gap >= 0) & (gap < WIN)
                for head in range(heads):
                    columns = slice(head * HS, (head + 1) * HS)
                    key = kv_ref[low : low + KEY_TILE, head * 2 * HS : head * 2 * HS + HS]
                    value = kv_ref[low : low + KEY_TILE, head * 2 * HS + HS : (head + 1) * 2 * HS]
                    scores = lax.dot_general(
                        query[:, columns],
                        key,
                        (((1,), (1,)), ((), ())),
                        preferred_element_type=jnp.float32,
                    )
                    weights = jnp.where(usable, jnp.exp2(scores * scale), 0.0)
                    den[:, columns] += weights[:, :HS] + weights[:, HS:]
                    num[:, columns] += jnp.dot(
                        weights.astype(jnp.bfloat16), value, preferred_element_type=jnp.float32
                    )

    if finish:
        parts = []
        for head in range(heads):
            columns = slice(head * HS, (head + 1) * HS)
            total = jnp.sum(den[:, columns], axis=1, keepdims=True)
            parts.append((num[:, columns] / total).astype(jnp.bfloat16))
        attended = jnp.concatenate(parts, axis=1)
        out[...] = jnp.dot(
            attended, out_weight[...], preferred_element_type=jnp.float32
        ).astype(jnp.bfloat16)


def attend(distances, scalars, ends, query, byte_patch, blocks, sums=None, out_weight=None):
    rows, width = query.shape
    heads = width // HS
    tile = rows // (ends.shape[0] // 2)
    start, finish = sums is None, out_weight is not None
    smem = pl.BlockSpec(memory_space=pltpu.SMEM)
    tiled = lambda columns: pl.BlockSpec((tile, columns), lambda i: (i, 0))
    whole = lambda array: pl.BlockSpec(array.shape, lambda i: (0, 0))
    operands = [scalars, ends, query, byte_patch, *blocks]
    in_specs = [smem, smem, tiled(width), tiled(1)] + [whole(block) for block in blocks]
    if not start:
        operands += list(sums)
        in_specs += [tiled(width), tiled(width)]
    if finish:
        operands.append(out_weight)
        in_specs.append(whole(out_weight))
        out_shape = jax.ShapeDtypeStruct((rows, out_weight.shape[1]), jnp.bfloat16)
        out_specs = tiled(out_weight.shape[1])
        scratch = [pltpu.VMEM((tile, width), jnp.float32)] * 2
    else:
        out_shape = [jax.ShapeDtypeStruct((rows, width), jnp.float32)] * 2
        out_specs = [tiled(width)] * 2
        scratch = []
    keys = sum(block.shape[0] for block in blocks)
    return pl.pallas_call(
        functools.partial(attend_kernel, heads, distances, start, finish),
        grid=(rows // tile,),
        in_specs=in_specs,
        out_specs=out_specs,
        out_shape=out_shape,
        scratch_shapes=scratch,
        compiler_params=pltpu.CompilerParams(vmem_limit_bytes=48 * 2**20),
        cost_estimate=pl.CostEstimate(
            flops=8 * rows * keys * width, bytes_accessed=4 * keys * width, transcendentals=0
        ),
    )(*operands)


def on_device(
    patch_states,
    mlp_gain,
    up_weight,
    down_weight,
    kv_gain,
    kv_weight,
    byte_states,
    query_weight,
    out_weight,
    patch_counts,
    byte_patch,
):
    seq = lax.axis_size("seq")
    me = lax.axis_index("seq")
    patch_rows, features = patch_states.shape
    size = 4 if seq % 4 == 0 else 1
    groups = [[base + i for i in range(size)] for base in range(0, seq, size)]
    across = [[base + i for base in range(0, seq, size)] for i in range(size)]
    place = lax.rem(me, size)

    up_part = lax.all_to_all(up_weight, "seq", 1, 0, axis_index_groups=groups, tiled=True)
    down_part = lax.all_to_all(down_weight, "seq", 0, 1, axis_index_groups=groups, tiled=True)
    up_all = lax.all_gather(up_part, "seq", axis=0, tiled=True, axis_index_groups=across)
    down_all = lax.all_gather(down_part, "seq", axis=1, tiled=True, axis_index_groups=across)

    normed = scale_rows(patch_states.astype(jnp.float32), mlp_gain.astype(jnp.float32)).astype(
        jnp.bfloat16
    )
    tokens = lax.all_gather(normed, "seq", axis=0, tiled=True, axis_index_groups=groups)
    counts = lax.all_gather(patch_counts, "seq", axis=0, tiled=True)

    heads_here = kv_weight.shape[1] // (2 * HS)
    bytes_here = byte_states.shape[0]
    query_proj = jnp.dot(byte_states, query_weight, preferred_element_type=jnp.float32).reshape(
        bytes_here, heads_here, HS
    )
    queries = unit_rows(query_proj).astype(jnp.bfloat16).reshape(bytes_here, heads_here * HS)

    preact = jnp.dot(tokens, up_all, preferred_element_type=jnp.float32)
    hidden = jax.nn.gelu(preact, approximate=False).astype(jnp.bfloat16)
    partial_value = jnp.dot(hidden, down_all, preferred_element_type=jnp.float32).astype(
        jnp.bfloat16
    )
    part = sum_over_cores(partial_value, 1).astype(jnp.bfloat16)
    part = part.reshape(size, patch_rows, part.shape[1])
    mixed = lax.dynamic_index_in_dim(part, place, 0, keepdims=False).astype(jnp.float32)
    for turn in range(1, size):
        pairs = [(base + i, base + (i ^ turn)) for base in range(0, seq, size) for i in range(size)]
        piece = lax.dynamic_index_in_dim(part, lax.bitwise_xor(place, turn), 0, keepdims=False)
        mixed = mixed + lax.ppermute(piece, "seq", pairs).astype(jnp.float32)
    mixed = join_cores(mixed.astype(jnp.bfloat16), 1).astype(jnp.float32)

    kv_in = scale_rows(
        patch_states.astype(jnp.float32) + mixed, kv_gain.astype(jnp.float32)
    ).astype(jnp.bfloat16)
    projected = jnp.dot(kv_in, kv_weight, preferred_element_type=jnp.float32).reshape(
        patch_rows, heads_here, 2, HS
    )
    kv_pack = (
        jnp.stack([unit_rows(projected[:, :, 0]), projected[:, :, 1]], axis=2)
        .astype(jnp.bfloat16)
        .reshape(patch_rows, heads_here * 2 * HS)
    )

    fewest = patch_rows // 2
    depth = (WIN + fewest - 2) // fewest
    own_count = patch_counts[0]
    blocks = [kv_pack]
    scalars = [jnp.zeros((), jnp.int32), own_count]
    first = jnp.zeros((), jnp.int32)
    for back in range(1, depth + 1):
        need = min(patch_rows, -(-(WIN - 1 - (back - 1) * fewest) // KEY_TILE) * KEY_TILE)
        source = kv_pack
        if need <= fewest:
            source = lax.dynamic_slice_in_dim(kv_pack, own_count - need, need, 0)
        blocks.append(
            lax.ppermute(source, "seq", [(i, i + back) for i in range(max(0, seq - back))])
        )
        held = jnp.where(me >= back, counts[jnp.maximum(me - back, 0)], 0)
        first = first - held
        if need <= fewest:
            scalars += [first + held - need, jnp.where(me >= back, need, 0)]
        else:
            scalars += [first, held]
    scalars = jnp.stack(scalars).astype(jnp.int32)
    tile = min(256, bytes_here)
    by_tile = byte_patch.reshape(bytes_here // tile, tile)
    ends = jnp.stack([by_tile[:, 0], by_tile[:, -1]], axis=1).reshape(-1)
    columns = byte_patch[:, None]
    sums = attend((0,), scalars, ends, queries, columns, blocks[:1])
    for back in range(1, depth):
        sums = attend((back,), scalars, ends, queries, columns, blocks[back : back + 1], sums)
    term = attend((depth,), scalars, ends, queries, columns, blocks[depth:], sums, out_weight)
    return sum_over_cores(term, 0).astype(jnp.bfloat16)


def solution(mesh):
    in_specs = (
        P("seq", None),
        P(),
        P("seq", "mp"),
        P("mp", "seq"),
        P(),
        P(None, "mp"),
        P("seq", None),
        P(None, "mp"),
        P("mp", None),
        P("seq"),
        P("seq"),
    )
    out_specs = P(("seq", "mp"), None)
    return jax.shard_map(
        on_device, mesh=mesh, in_specs=in_specs, out_specs=out_specs, check_vma=False
    )
```

time: 624 us -> 553 us (0.89)
  waiting for transfers between devices: 416 us -> 268 us
  blocking collectives: 35.5 us -> 69.8 us
  Pallas kernels: 0 us -> 33.6 us
  matrix products: 74.5 us -> 45 us
  starting transfers between devices: 12.5 us -> 37.4 us
  local copies, waits for them, and re-layouts: 25.3 us -> 38.4 us
  loops' own time: 9.68 us -> 0 us
    all_gather x2 -> x3, waiting for transfers between devices: 320 us -> 213 us  [the longest x1 90.6 us: on_device(): lax.all_gather(normed, 'seq', axis=0, tiled=True, axis_index_groups=groups)]
    pallas_call x0 -> x5, Pallas kernels: none -> 33.6 us  [attend(): pl.pallas_call(functools.partial(attend_kernel, heads, distances, start,...]
    unnamed x1, blocking collectives: 9.84 us -> 41.1 us
    all_to_all x0 -> x2, blocking collectives: none -> 28.7 us  [the longest x1 15.1 us: on_device(): lax.all_to_all(up_weight, 'seq', 1, 0, axis_index_groups=groups, tiled=True)]
    dot_general x12 -> x1, matrix products: 64.1 us -> 37.2 us  [on_device(): jnp.dot(hidden, down_all, preferred_element_type=jnp.float32)]
    all_gather x1 -> x0, blocking collectives: 25.7 us -> none  [entering(): pieces = jax.tree.map(lambda part: lax.all_gather(part, axis), value)]
    ppermute x4 -> x10, starting transfers between devices: 12.4 us -> 37.3 us  [the longest x4 30.1 us: on_device(): lax.ppermute(source, 'seq', [(i, i + back) for i in range(max(0, seq - ba...]
    ppermute x4 -> x10, waiting for transfers between devices: 78 us -> 55 us  [the longest x3 45.4 us: on_device(): mixed = mixed + lax.ppermute(piece, 'seq', pairs).astype(jnp.float32)]
  transfers between devices with their start and end apart: 8 -> 13, of which waited for: 5 -> 8; matrix products, arithmetic and copies ran while one was open for 10% -> 4% of each run, Pallas kernels for 0% -> 5%
where the time goes in v1:
time: 553 us; the launch traced here: 544 us
  waiting for transfers between devices  268 us (48%)
  blocking collectives  69.8 us (13%)
  matrix products  45 us (8%)
  local copies, waits for them, and re-layouts  38.4 us (7%)
  starting transfers between devices  37.4 us (7%)
  other arithmetic  35.4 us (6%)
  Pallas kernels  33.6 us (6%)
  between operations  16.3 us (3%)
    all_gather x1, waiting for transfers between devices, on_device(): lax.all_gather(normed, 'seq', axis=0, tiled=True, axis_index_groups=groups)  90.6 us
    all_gather x1, waiting for transfers between devices, on_device(): lax.all_gather(down_part, 'seq', axis=1, tiled=True, axis_index_groups=ac...  72.3 us
    all_gather x1, waiting for transfers between devices, on_device(): lax.all_gather(up_part, 'seq', axis=0, tiled=True, axis_index_groups=across)  50.4 us
    ppermute x3, waiting for transfers between devices, on_device(): mixed = mixed + lax.ppermute(piece, 'seq', pairs).astype(jnp.float32)  45.4 us
    unnamed x1, blocking collectives  41.1 us
    dot_general x1, matrix products, on_device(): jnp.dot(hidden, down_all, preferred_element_type=jnp.float32)  37.2 us
    pallas_call x5, Pallas kernels, attend(): pl.pallas_call(functools.partial(attend_kernel, heads, distances, start,...  33.6 us
    ppermute x4, starting transfers between devices, on_device(): lax.ppermute(source, 'seq', [(i, i + back) for i in range(max(0, seq - ba...  30.1 us
  transfers between devices with their start and end apart: 13, of which 8 were waited for; matrix products, arithmetic and copies ran while one was open for 4% of the time, Pallas kernels for 5%

profile of v1, /device:TPU:9, one launch (start us, length us, event | category | flops | bytes accessed | tf_op | source)
XLA Modules:
  0.0 544.2 jit_solution(10934637143769632686)
XLA Ops:
  6.5 2.4 copy.51
  8.9 15.1 %all_to_all.38 = bf16[128,4,896]{0,2,1:T(8,128)(2,1)S(1)} all-to-all(bf16[128,4,896]{0,2,1:T(8,128)(2,1)} %bitcast.50), channel_id=1, replica_groups={{0,2,4,6},{8,10,12,14},{16,18,20,22},{24,26,28,30},{1,3,5,7},{9,11,13,1..., dimensions={1} | all-to-all | bytes 1835008 | tf_op jit(solution)/shard_map/all_to_all | solution.py:165
  24.0 1.3 copy.52
  25.4 13.5 %all_to_all.39 = bf16[4,896,128]{2,1,0:T(8,128)(2,1)S(1)} all-to-all(bf16[4,896,128]{2,1,0:T(8,128)(2,1)} %bitcast.52), channel_id=1, replica_groups={{0,2,4,6},{8,10,12,14},{16,18,20,22},{24,26,28,30},{1,3,5,7},{9,11,13,1..., dimensions={0} | all-to-all | bytes 1835008 | tf_op jit(solution)/shard_map/all_to_all | solution.py:166
  38.9 1.3 copy.53
  40.3 2.1 fusion.10
  42.3 3.5 fusion.12
  45.9 50.4 %all-gather.6.cloned.1.call-done = bf16[2048,896]{1,0:T(8,128)(2,1)} async-done(((bf16[512,896]{1,0:T(8,128)(2,1)}), bf16[2048,896]{1,0:T(8,128)(2,1)}) %all-gather.6.cloned.1.call-update) | async-done | bytes 3670032 | tf_op jit(solution)/shard_map/all_gather | solution.py:167
  96.2 72.3 %all-gather.8.cloned.1.call-done = bf16[896,2048]{0,1:T(8,128)(2,1)} async-done(((bf16[896,512]{0,1:T(8,128)(2,1)}), bf16[896,2048]{0,1:T(8,128)(2,1)}) %all-gather.8.cloned.1.call-update) | async-done | bytes 3670032 | tf_op jit(solution)/shard_map/all_gather | solution.py:168
  168.6 90.6 %all-gather.4.cloned.1.call-done = bf16[2048,2048]{1,0:T(8,128)(2,1)} async-done(((bf16[512,2048]{1,0:T(8,128)(2,1)}), bf16[2048,2048]{1,0:T(8,128)(2,1)}) %all-gather.4.cloned.1.call-update) | async-done | bytes 8388624 | tf_op jit(solution)/shard_map/all_gather | solution.py:173
  259.1 37.2 %convolution_convert_fusion = bf16[2048,2048]{1,0:T(8,128)(2,1)} fusion(bf16[896,2048]{0,1:T(8,128)(2,1)} %all-gather.8.cloned.1.call-done, bf16[2048,2048]{1,0:T(8,128)(2,1)} %all-gather.4.cloned.1.call-done, bf16[2048,896]{1,0:T(8,128)(2,1)} %all-gather.6.cloned.1.call-done), kind=kOutput, calls=%fused_computation.2 | convolution fusion | flops 15155855360 | bytes 24117248 | tf_op jit(solution)/shard_map/dot_general | solution.py:185
  296.4 4.6 constant_dynamic-slice_fusion.2
  300.9 0.7 collective-permute-start
  301.6 7.1 %collective-permute-done = bf16[2048,1024]{1,0:T(8,128)(2,1)} collective-permute-done((bf16[2048,1024]{1,0:T(8,128)(2,1)}, bf16[2048,1024]{1,0:T(8,128)(2,1)}, u32[]{:S(2)}, u32[]{:S(2)}) %collective-permute-start) | collective-permute-done | bytes 4194336 | tf_op jit(solution)/shard_map/ppermute | solution.py:34
  308.7 5.6 %add_convert_fusion = bf16[2048,1024]{1,0:T(8,128)(2,1)S(1)} fusion(bf16[2048,1024]{1,0:T(8,128)(2,1)} %collective-permute-done, bf16[2048,2048]{1,0:T(8,128)(2,1)} %convolution_convert_fusion, s32[]{:T(128)S(6)} %select_n.64), kind=kLoop, calls=%fused_computation.1 | loop fusion | flops 8388608 | bytes 12582916 | tf_op jit(solution)/shard_map/convert_element_type | solution.py:188
  314.3 1.9 copy-done.9
  316.3 1.8 dynamic-slice_bitcast_fusion.2
  318.0 1.2 collective-permute-start.1
  319.2 0.3 collective-permute-start.2
  319.5 1.2 collective-permute-start.3
  320.7 22.0 %collective-permute-done.1 = bf16[512,1024]{1,0:T(8,128)(2,1)} collective-permute-done((bf16[512,1024]{1,0:T(8,128)(2,1)}, bf16[512,1024]{1,0:T(8,128)(2,1)}, u32[]{:S(2)}, u32[]{:S(2)}) %collective-permute-start.1) | collective-permute-done | bytes 1048608 | tf_op jit(solution)/shard_map/ppermute | solution.py:194
  342.7 0.9 collective-permute-done.2
  343.6 22.6 %collective-permute-done.3 = bf16[512,1024]{1,0:T(8,128)(2,1)} collective-permute-done((bf16[512,1024]{1,0:T(8,128)(2,1)S(1)}, bf16[512,1024]{1,0:T(8,128)(2,1)}, u32[]{:S(2)}, u32[]{:S(2)}) %collective-permute-start.3) | collective-permute-done | bytes 1048608 | tf_op jit(solution)/shard_map/ppermute | solution.py:194
  366.1 3.1 fusion.48
  369.2 1.5 collective-permute-start.4
  370.7 4.0 bitcast_reduce_fusion
  374.7 1.5 broadcast_select_fusion.1
  376.2 0.8 multiply_reduce_fusion
  377.0 0.2 copy-done.14
  377.2 3.8 fusion.44
  381.0 4.2 reshape.69
  385.2 5.5 %multiply_reduce_fusion.1 = f32[512,4]{1,0:T(8,128)S(1)} fusion(f32[512,4,2,128]{3,2,1,0:T(2,128)} %reshape.69), kind=kLoop, calls=%fused_computation.74 | loop fusion | flops 522240 | bytes 1056768 | tf_op jit(solution)/shard_map/reduce_sum | solution.py:21
  390.8 2.7 slice.24
  393.5 5.2 multiply_convert_fusion.2
  398.7 3.2 pad_maximum_fusion.2
  402.0 1.8 convert_element_type.88.refs_0_
  403.7 2.2 collective-permute-start.8
  406.0 3.1 collective-permute-start.7
  409.8 0.6 dynamic-slice
  410.4 0.8 dynamic-update-slice
  411.2 41.1 %all-reduce = s32[16]{0:T(128)S(1)} all-reduce(s32[16]{0:T(128)S(1)} %dynamic-update-slice), channel_id=1, replica_groups=mesh['seq'=16,'mp'=2] {'seq'}, use_global_device_ids=true, to_apply=%add | all-reduce | flops 16 | bytes 128
  452.3 0.7 fusion.83
  453.6 1.0 copy.49
  454.6 2.9 copy.50
  457.7 1.0 copy.60.byte_patch
  459.9 0.1 stack.43.scalars
  460.0 22.9 %collective-permute-start.6 = (bf16[512,1024]{1,0:T(8,128)(2,1)S(1)}, bf16[512,1024]{1,0:T(8,128)(2,1)S(1)}, u32[]{:S(2)}, u32[]{:S(2)}) collective-permute-start(bf16[512,1024]{1,0:T(8,128)(2,1)S(1)} %convert_element_type.88.refs_0_), channel_id=1, source_target_pairs={{0,6},{2,8},{4,10},{6,12},{8,14},{10,16},{12,18},{14,20},{16,22},{... | collective-permute-start | bytes 3145736 | tf_op jit(solution)/shard_map/ppermute | solution.py:221
  482.9 2.2 mul.97
  485.1 1.9 fusion.45.query
  487.1 0.1 constant_dynamic-slice_fusion.1
  487.2 1.9 collective-permute-start.5
  489.1 5.4 %shard_map.109 = (f32[1024,512]{1,0:T(8,128)S(1)}, f32[1024,512]{1,0:T(8,128)}) custom-call(s32[10]{0:T(128)S(1)} %stack.43.scalars, s32[8]{0:T(128)S(1)} %reshape.67.ends, bf16[1024,512]{1,0:T(8,128)(2,1)S(1)} %fusion.45.query, s32[1024,1]{1,0:T(8,128)S(1)} %copy-done.3, bf16[512,1024]{1,0:T(8,128)(2,1)S(1)} %convert_element_type.88.refs_0_), custom_call_target="tpu_custom_call" | custom-call | flops 2147483648 | bytes 1048576 | tf_op jit(solution)/shard_map/pallas_call | solution.py:130
  494.6 1.4 copy-done.7
  496.0 8.3 %shard_map.110 = (f32[1024,512]{1,0:T(8,128)S(1)}, f32[1024,512]{1,0:T(8,128)}) custom-call(s32[10]{0:T(128)S(1)} %stack.43.scalars, s32[8]{0:T(128)S(1)} %reshape.67.ends, bf16[1024,512]{1,0:T(8,128)(2,1)S(1)} %fusion.45.query, s32[1024,1]{1,0:T(8,128)S(1)} %copy-done.3, bf16[512,1024]{1,0:T(8,128)(2,1)} %collective-permute-done.8.refs_0_, ...), custom_call_target="tpu_custom_call" | custom-call | flops 2147483648 | bytes 1048576 | tf_op jit(solution)/shard_map/pallas_call | solution.py:130
  504.3 1.4 copy-done.6
  505.6 8.3 %shard_map.111 = (f32[1024,512]{1,0:T(8,128)S(1)}, f32[1024,512]{1,0:T(8,128)}) custom-call(s32[10]{0:T(128)S(1)} %stack.43.scalars, s32[8]{0:T(128)S(1)} %reshape.67.ends, bf16[1024,512]{1,0:T(8,128)(2,1)S(1)} %fusion.45.query, s32[1024,1]{1,0:T(8,128)S(1)} %copy-done.3, bf16[512,1024]{1,0:T(8,128)(2,1)} %collective-permute-done.7.refs_0_, ...), custom_call_target="tpu_custom_call" | custom-call | flops 2147483648 | bytes 1048576 | tf_op jit(solution)/shard_map/pallas_call | solution.py:130
  514.0 1.4 copy-done.5
  515.3 7.2 %shard_map.112 = (f32[1024,512]{1,0:T(8,128)S(1)}, f32[1024,512]{1,0:T(8,128)}) custom-call(s32[10]{0:T(128)S(1)} %stack.43.scalars, s32[8]{0:T(128)S(1)} %reshape.67.ends, bf16[1024,512]{1,0:T(8,128)(2,1)S(1)} %fusion.45.query, s32[1024,1]{1,0:T(8,128)S(1)} %copy-done.3, bf16[512,1024]{1,0:T(8,128)(2,1)S(1)} %collective-permute-done.6.refs_0_, ...), custom_call_target="tpu_custom_call" | custom-call | flops 2147483648 | bytes 1048576 | tf_op jit(solution)/shard_map/pallas_call | solution.py:130
  522.6 1.3 copy-done.2
  523.9 4.3 shard_map.113
  528.2 1.3 copy-done.1
  529.6 2.4 collective-permute-start.9
  531.9 2.4 collective-permute-done.9
  534.3 2.9 add_convert_fusion.1
  (48 shorter events, 0.6 us)
Async XLA Ops:
  6.5 364.2 %copy-start = (bf16[1024,1024]{1,0:T(8,128)(2,1)S(1)}, bf16[1024,1024]{1,0:T(8,128)(2,1)}, u32[]{:S(2)}) copy-start(bf16[1024,1024]{1,0:T(8,128)(2,1)} %param.17) | copy-start | bytes 6291460
  6.5 89.7 %all-gather.6.cloned.1.call-start = ((), (), s32[]{:S(2)}) async-start(), calls=%async_computation.3 | async-start | bytes 4587520 | tf_op jit(solution)/shard_map/all_gather | solution.py:167
  8.9 31.3 %copy-start.12 = (bf16[2048]{0:T(1024)(128)(2,1)S(1)}, bf16[2048]{0:T(1024)(128)(2,1)}, u32[]{:S(2)}) copy-start(bf16[2048]{0:T(1024)(128)(2,1)} %param.12) | copy-start | bytes 12292
  25.3 143.2 %all-gather.8.cloned.1.call-start = ((), (), s32[]{:S(2)}) async-start(), calls=%async_computation.4 | async-start | bytes 4587520 | tf_op jit(solution)/shard_map/all_gather | solution.py:168
  40.2 219.0 %all-gather.4.cloned.1.call-start = ((), (), s32[]{:S(2)}) async-start(), calls=%async_computation.2 | async-start | bytes 10485760 | tf_op jit(solution)/shard_map/all_gather | solution.py:173
  300.9 7.8 %collective-permute-start = (bf16[2048,1024]{1,0:T(8,128)(2,1)}, bf16[2048,1024]{1,0:T(8,128)(2,1)}, u32[]{:S(2)}, u32[]{:S(2)}) collective-permute-start(bf16[2048,1024]{1,0:T(8,128)(2,1)} %constant_dynamic-slice_fusion.2), channel_id=1, source_target_pairs={{0,1},{1,0},{2,3},{3,2},{4,5},{5,4},{6,7},{7,6},{8,9},{9,8},{10,11... | collective-permute-start | bytes 12582920 | tf_op jit(solution)/shard_map/ppermute | solution.py:34
  314.3 2.0 copy-start.9
  318.0 52.7 %copy-start.13 = (bf16[2048]{0:T(1024)(128)(2,1)S(1)}, bf16[2048]{0:T(1024)(128)(2,1)}, u32[]{:S(2)}) copy-start(bf16[2048]{0:T(1024)(128)(2,1)} %param.15) | copy-start | bytes 12292
  318.0 24.7 %collective-permute-start.1 = (bf16[512,1024]{1,0:T(8,128)(2,1)}, bf16[512,1024]{1,0:T(8,128)(2,1)}, u32[]{:S(2)}, u32[]{:S(2)}) collective-permute-start(bf16[512,1024]{1,0:T(8,128)(2,1)} %get-tuple-element.21), channel_id=1, source_target_pairs={{0,2},{2,0},{4,6},{6,4},{8,10},{10,8},{12,14},{14,12},{16,18},{18,... | collective-permute-start | bytes 3145736 | tf_op jit(solution)/shard_map/ppermute | solution.py:194
  319.2 24.4 %collective-permute-start.2 = (bf16[512,1024]{1,0:T(8,128)(2,1)}, bf16[512,1024]{1,0:T(8,128)(2,1)}, u32[]{:S(2)}, u32[]{:S(2)}) collective-permute-start(bf16[512,1024]{1,0:T(8,128)(2,1)} %get-tuple-element.23), channel_id=1, source_target_pairs={{0,4},{2,6},{4,0},{6,2},{8,12},{10,14},{12,8},{14,10},{16,20},{18,... | collective-permute-start | bytes 3145736 | tf_op jit(solution)/shard_map/ppermute | solution.py:194
  319.5 46.6 %collective-permute-start.3 = (bf16[512,1024]{1,0:T(8,128)(2,1)S(1)}, bf16[512,1024]{1,0:T(8,128)(2,1)}, u32[]{:S(2)}, u32[]{:S(2)}) collective-permute-start(bf16[512,1024]{1,0:T(8,128)(2,1)S(1)} %get-tuple-element.22), channel_id=1, source_target_pairs={{0,6},{2,4},{4,2},{6,0},{8,14},{10,12},{12,10},{14,8},{16,22},{18,... | collective-permute-start | bytes 3145736 | tf_op jit(solution)/shard_map/ppermute | solution.py:194
  369.2 5.5 %collective-permute-start.4 = (bf16[512,1024]{1,0:T(8,128)(2,1)S(1)}, bf16[512,1024]{1,0:T(8,128)(2,1)}, u32[]{:S(2)}, u32[]{:S(2)}) collective-permute-start(bf16[512,1024]{1,0:T(8,128)(2,1)S(1)} %fusion.48), channel_id=1, source_target_pairs={{0,1},{1,0},{2,3},{3,2},{4,5},{5,4},{6,7},{7,6},{8,9},{9,8},{10,11... | collective-permute-start | bytes 3145736 | tf_op jit(solution)/shard_map/ppermute | solution.py:43
  370.7 5.5 %copy-start.8 = (bf16[512,2048]{1,0:T(8,128)(2,1)S(1)}, bf16[512,2048]{1,0:T(8,128)(2,1)}, u32[]{:S(2)}) copy-start(bf16[512,2048]{1,0:T(8,128)(2,1)} %param.11) | copy-start | bytes 6291460
  374.7 2.5 copy-start.14
  385.2 8.3 %copy-start.10 = (f32[512,4,2,128]{3,2,1,0:T(2,128)S(1)}, f32[512,4,2,128]{3,2,1,0:T(2,128)}, u32[]{:S(2)}) copy-start(f32[512,4,2,128]{3,2,1,0:T(2,128)} %reshape.69) | copy-start | bytes 6291460
  393.4 12.6 %copy-start.11 = (s32[1024]{0:T(1024)S(1)}, s32[1024]{0:T(1024)}, u32[]{:S(2)}) copy-start(s32[1024]{0:T(1024)} %param.21) | copy-start | bytes 12292
  393.4 16.4 %copy-start.15 = (u32[32]{0:T(128)S(1)}, u32[32]{0:T(128)}, u32[]{:S(2)}) copy-start(u32[32]{0:T(128)} %constant.137) | copy-start | bytes 388
  403.7 92.2 %collective-permute-start.8 = (bf16[512,1024]{1,0:T(8,128)(2,1)S(1)}, bf16[512,1024]{1,0:T(8,128)(2,1)}, u32[]{:S(2)}, u32[]{:S(2)}) collective-permute-start(bf16[512,1024]{1,0:T(8,128)(2,1)S(1)} %convert_element_type.88.refs_0_), channel_id=1, source_target_pairs={{0,2},{2,4},{4,6},{6,8},{8,10},{10,12},{12,14},{14,16},{16,18},{18... | collective-permute-start | bytes 3145736 | tf_op jit(solution)/shard_map/ppermute | solution.py:221
  406.0 99.6 %collective-permute-start.7 = (bf16[512,1024]{1,0:T(8,128)(2,1)S(1)}, bf16[512,1024]{1,0:T(8,128)(2,1)}, u32[]{:S(2)}, u32[]{:S(2)}) collective-permute-start(bf16[512,1024]{1,0:T(8,128)(2,1)S(1)} %convert_element_type.88.refs_0_), channel_id=1, source_target_pairs={{0,4},{2,6},{4,8},{6,10},{8,12},{10,14},{12,16},{14,18},{16,20},{1... | collective-permute-start | bytes 3145736 | tf_op jit(solution)/shard_map/ppermute | solution.py:221
  460.0 29.1 %copy-start.3 = (s32[1024,1]{1,0:T(8,128)S(1)}, s32[1024,1]{1,0:T(8,128)}, u32[]{:S(2)}) copy-start(s32[1024,1]{1,0:T(8,128)} %copy.60.byte_patch) | copy-start | bytes 12292
  460.0 55.3 %collective-permute-start.6 = (bf16[512,1024]{1,0:T(8,128)(2,1)S(1)}, bf16[512,1024]{1,0:T(8,128)(2,1)S(1)}, u32[]{:S(2)}, u32[]{:S(2)}) collective-permute-start(bf16[512,1024]{1,0:T(8,128)(2,1)S(1)} %convert_element_type.88.refs_0_), channel_id=1, source_target_pairs={{0,6},{2,8},{4,10},{6,12},{8,14},{10,16},{12,18},{14,20},{16,22},{... | collective-permute-start | bytes 3145736 | tf_op jit(solution)/shard_map/ppermute | solution.py:221
  487.2 36.7 %collective-permute-start.5 = (bf16[256,1024]{1,0:T(8,128)(2,1)S(1)}, bf16[256,1024]{1,0:T(8,128)(2,1)S(1)}, u32[]{:S(2)}, u32[]{:S(2)}) collective-permute-start(bf16[256,1024]{1,0:T(8,128)(2,1)S(1)} %constant_dynamic-slice_fusion.1), channel_id=1, source_target_pairs={{0,8},{2,10},{4,12},{6,14},{8,16},{10,18},{12,20},{14,22},{16,24},... | collective-permute-start | bytes 1572872 | tf_op jit(solution)/shard_map/ppermute | solution.py:221
  494.6 1.4 copy-start.7
  504.3 1.4 copy-start.6
  513.9 1.4 copy-start.5
  515.3 8.5 %copy-start.4 = (bf16[512,1024]{1,0:T(8,128)(2,1)S(1)}, bf16[512,1024]{1,0:T(8,128)(2,1)}, u32[]{:S(2)}) copy-start(bf16[512,1024]{1,0:T(8,128)(2,1)} %refs_3_.1) | copy-start | bytes 3145732
  522.6 1.3 copy-start.2
  528.1 1.3 copy-start.1
  529.6 4.8 collective-permute-start.9
Sparse Core Ops, SparseCore 0:
  25.4 70.7 all-gather.5
  97.8 70.7 all-gather.7
  170.4 88.6 all-gather.3

commit v2 on v1

--- a/solution.py
+++ b/solution.py
@@ -11,6 +11,8 @@
 HS = 128
 WIN = 1024
 KEY_TILE = 256
+PLANE = 4
+TILE = 128
 
 
 def scale_rows(values, gain):
@@ -44,6 +46,384 @@
     first = jnp.where(me == 0, value, got)
     second = jnp.where(me == 0, got, value)
     return jnp.concatenate([first, second], axis=dim)
+
+
+def block_kernel(
+    patch, mlp_gain, up, down, kv_gain, kv_weight, byte_states, query_weight,
+    kv_out, query_out,
+    up_all, down_all, tokens, hidden, core_send, core_got, kept, plane_send, plane_got, mixed,
+    swap_send, swap_recv, chunk_recv, right_send, left_send,
+    token_send, token_recv, half_send, half_recv,
+    core_sems, plane_sems, plane_recv, mixed_send, mixed_recv, local_sems,
+):
+    seq, core = lax.axis_index("seq"), lax.axis_index("mp")
+    depth = lax.axis_size("seq") // PLANE
+    z, place = seq // PLANE, lax.rem(seq, PLANE)
+    y, x = place // 2, lax.rem(place, 2)
+    rows, features = patch.shape
+    thin = up.shape[0]
+    units = up_all.shape[1]
+    half = features // 2
+    wide = features // (2 * depth)
+    MESH = pl.DeviceIdType.MESH
+
+    def member(turn):
+        return 2 * lax.rem(y + turn // 2, 2) + lax.rem(x + lax.rem(turn, 2), 2)
+
+    def peer(turn):
+        return (z * PLANE + member(turn), core)
+
+    partner = (seq, 1 - core)
+
+    barrier = pltpu.get_barrier_semaphore()
+    for turn in range(1, PLANE):
+        pl.semaphore_signal(barrier, inc=1, device_id=peer(turn), device_id_type=MESH)
+    pl.semaphore_signal(barrier, inc=1, device_id=partner, device_id_type=MESH)
+
+    @pl.when(z > 0)
+    def _():
+        pl.semaphore_signal(barrier, inc=1, device_id=(seq - PLANE, core), device_id_type=MESH)
+
+    @pl.when(z < depth - 1)
+    def _():
+        pl.semaphore_signal(barrier, inc=1, device_id=(seq + PLANE, core), device_id_type=MESH)
+
+    pl.semaphore_wait(
+        barrier, PLANE + jnp.where(z > 0, 1, 0) + jnp.where(z < depth - 1, 1, 0)
+    )
+
+    def remote(src, dst, send, recv, device):
+        return pltpu.make_async_remote_copy(
+            src_ref=src, dst_ref=dst, send_sem=send, recv_sem=recv, device_id=device,
+            device_id_type=MESH,
+        )
+
+    def chunk(kind, index):
+        if kind == 0:
+            return up_all.at[pl.ds(pl.multiple_of(index * thin, thin), thin), :]
+        return down_all.at[index]
+
+    def held(kind, owner):
+        start = pl.multiple_of(owner * units, units)
+        if kind == 0:
+            return up.at[:, pl.ds(start, units)]
+        return down.at[pl.ds(start, units), :]
+
+    def swap(kind, turn):
+        index = z * PLANE + place
+        return remote(
+            held(kind, member(turn)), chunk(kind, index), swap_send.at[kind, turn],
+            swap_recv.at[kind, turn], peer(turn),
+        )
+
+    def swap_arrives(kind, turn):
+        index = z * PLANE + member(turn)
+        return remote(
+            chunk(kind, index), chunk(kind, index), swap_send.at[kind, turn],
+            swap_recv.at[kind, turn], peer(turn),
+        )
+
+    def pass_right(kind, index):
+        return remote(
+            chunk(kind, index), chunk(kind, index), right_send.at[kind, index],
+            chunk_recv.at[kind, index], (seq + PLANE, core),
+        )
+
+    def pass_left(kind, index):
+        return remote(
+            chunk(kind, index), chunk(kind, index), left_send.at[kind, index],
+            chunk_recv.at[kind, index], (seq - PLANE, core),
+        )
+
+    def spread(kind, index):
+        @pl.when(z < depth - 1)
+        def _():
+            pass_right(kind, index).start()
+
+        @pl.when(z > 0)
+        def _():
+            pass_left(kind, index).start()
+
+    def hop(kind, step):
+        far, turn = step // PLANE, lax.rem(step, PLANE)
+
+        @pl.when(z - 1 - far >= 0)
+        def _():
+            index = (z - 1 - far) * PLANE + member(turn)
+            pass_left(kind, index).wait_recv()
+
+            @pl.when(z < depth - 1)
+            def _():
+                pass_right(kind, index).start()
+
+        @pl.when(z + 1 + far < depth)
+        def _():
+            index = (z + 1 + far) * PLANE + member(turn)
+            pass_right(kind, index).wait_recv()
+
+            @pl.when(z > 0)
+            def _():
+                pass_left(kind, index).start()
+
+    own = [
+        pltpu.make_async_copy(held(kind, place), chunk(kind, seq), local_sems.at[kind])
+        for kind in range(2)
+    ]
+    for kind in range(2):
+        own[kind].start()
+    for turn in range(1, PLANE):
+        swap(0, turn).start()
+    own[0].wait()
+    spread(0, seq)
+
+    gain = mlp_gain[...].astype(jnp.float32)
+    row_start = pl.multiple_of(place * rows, rows)
+
+    @pl.loop(0, rows // TILE)
+    def _(tile):
+        low = pl.multiple_of(tile * TILE, TILE)
+        values = patch[pl.ds(low, TILE), :].astype(jnp.float32)
+        tokens[pl.ds(row_start + low, TILE), :] = scale_rows(values, gain).astype(jnp.bfloat16)
+
+    for turn in range(1, PLANE):
+        swap_arrives(0, turn).wait_recv()
+        spread(0, z * PLANE + member(turn))
+    for turn in range(1, PLANE):
+        swap(1, turn).start()
+
+    def token_part(owner, side):
+        return tokens.at[
+            pl.ds(pl.multiple_of(owner * rows, rows), rows),
+            pl.ds(pl.multiple_of(side * half, half), half),
+        ]
+
+    def send_tokens(turn):
+        return remote(
+            token_part(place, core), token_part(place, core), token_send.at[turn],
+            token_recv.at[turn], peer(turn),
+        )
+
+    def tokens_arrive(turn):
+        part = token_part(member(turn), core)
+        return remote(part, part, token_send.at[turn], token_recv.at[turn], peer(turn))
+
+    def half_over(turn):
+        part = token_part(member(turn), core)
+        return remote(part, part, half_send.at[turn], half_recv.at[turn], partner)
+
+    def half_arrives(turn):
+        part = token_part(member(turn), 1 - core)
+        return remote(part, part, half_send.at[turn], half_recv.at[turn], partner)
+
+    for turn in range(1, PLANE):
+        send_tokens(turn).start()
+
+    heads = query_weight.shape[1] // HS
+    query_rows = byte_states.shape[0] // PLANE
+
+    @pl.loop(0, PLANE)
+    def _(step):
+        low = pl.multiple_of(step * query_rows, query_rows)
+        product = jnp.dot(
+            byte_states[pl.ds(low, query_rows), :], query_weight[...],
+            preferred_element_type=jnp.float32,
+        )
+        for head in range(heads):
+            columns = slice(head * HS, (head + 1) * HS)
+            query_out[pl.ds(low, query_rows), columns] = unit_rows(product[:, columns]).astype(
+                jnp.bfloat16
+            )
+        hop(0, step)
+
+    own[1].wait()
+    spread(1, seq)
+    for turn in range(1, PLANE):
+        swap_arrives(1, turn).wait_recv()
+        spread(1, z * PLANE + member(turn))
+
+    @pl.loop(PLANE, 2 * PLANE)
+    def _(step):
+        hop(0, step)
+
+    for turn in range(1, PLANE):
+        tokens_arrive(turn).wait_recv()
+        half_over(turn).start()
+
+    @pl.loop(2 * PLANE, (depth - 1) * PLANE)
+    def _(step):
+        hop(0, step)
+
+    for turn in range(1, PLANE):
+        half_arrives(turn).wait_recv()
+
+    tall = PLANE * rows // (2 * PLANE)
+
+    @pl.loop(0, 2 * PLANE)
+    def _(step):
+        low = pl.multiple_of(step * tall, tall)
+        preact = jnp.dot(
+            tokens[pl.ds(low, tall), :], up_all[...], preferred_element_type=jnp.float32
+        )
+        gelu = 0.5 * preact * (1.0 + lax.erf(preact * math.sqrt(0.5)))
+        hidden[pl.ds(low, tall), :] = gelu.astype(jnp.bfloat16)
+        hop(1, step)
+
+    near = jnp.minimum(z, depth - 1 - z)
+
+    def order(turn):
+        swapped = jnp.where((near == 1) & (turn < 2), 1 - turn, turn)
+        return jnp.where(z < depth // 2, swapped, depth - 1 - swapped)
+
+    def plane_out(turn, to):
+        start = pl.multiple_of(member(to) * rows, rows)
+        return remote(
+            plane_send.at[turn, pl.ds(start, rows), :], plane_got.at[turn, to],
+            plane_sems.at[turn, to], plane_recv.at[turn, to], peer(to),
+        )
+
+    def core_swap(turn):
+        return remote(
+            core_send, core_got.at[turn], core_sems.at[0, turn], core_sems.at[1, turn], partner
+        )
+
+    def product(turn, side, out):
+        chunks = order(turn) * PLANE + side * (PLANE // 2)
+        weight = jnp.concatenate([down_all[chunks + i] for i in range(PLANE // 2)], axis=1)
+
+        @pl.loop(0, PLANE)
+        def _(owner):
+            low = pl.multiple_of(owner * rows, rows)
+            out[pl.ds(low, rows), :] = jnp.dot(
+                hidden[pl.ds(low, rows), :], weight, preferred_element_type=jnp.float32
+            ).astype(jnp.bfloat16)
+
+    def one_block(turn):
+        product(turn, 1 - core, core_send)
+        core_swap(turn).start()
+        product(turn, core, kept)
+        core_swap(turn).wait()
+
+        @pl.loop(0, PLANE)
+        def _(owner):
+            low = pl.multiple_of(owner * rows, rows)
+            total = kept[pl.ds(low, rows), :].astype(jnp.float32) + core_got[
+                turn, pl.ds(low, rows), :
+            ].astype(jnp.float32)
+            plane_send[turn, pl.ds(low, rows), :] = total.astype(jnp.bfloat16)
+
+        for to in range(1, PLANE):
+            plane_out(turn, to).start()
+
+    @pl.loop(0, depth - 1)
+    def _(turn):
+        one_block(turn)
+
+    @pl.loop(2 * PLANE, (depth - 1) * PLANE)
+    def _(step):
+        hop(1, step)
+
+    one_block(depth - 1)
+
+    def mixed_over(turn, side):
+        part = mixed.at[2 * order(turn) + side]
+        return remote(part, part, mixed_send.at[turn], mixed_recv.at[turn], partner)
+
+    @pl.loop(0, depth)
+    def _(turn):
+        total = plane_send[turn, pl.ds(row_start, rows), :].astype(jnp.float32)
+        for to in range(1, PLANE):
+            plane_out(turn, to).wait_recv()
+            total = total + plane_got[turn, to].astype(jnp.float32)
+        mixed[2 * order(turn) + core] = total.astype(jnp.bfloat16)
+        mixed_over(turn, core).start()
+
+    @pl.loop(0, depth)
+    def _(turn):
+        mixed_over(turn, 1 - core).wait_recv()
+
+    later_gain = kv_gain[...].astype(jnp.float32)
+
+    @pl.loop(0, rows // TILE)
+    def _(tile):
+        low = pl.multiple_of(tile * TILE, TILE)
+        more = jnp.concatenate(
+            [mixed[i, pl.ds(low, TILE), :] for i in range(2 * depth)], axis=1
+        )
+        values = patch[pl.ds(low, TILE), :].astype(jnp.float32) + more.astype(jnp.float32)
+        kv_in = scale_rows(values, later_gain).astype(jnp.bfloat16)
+        projected = jnp.dot(kv_in, kv_weight[...], preferred_element_type=jnp.float32)
+        for head in range(heads):
+            key = slice(head * 2 * HS, head * 2 * HS + HS)
+            value = slice(head * 2 * HS + HS, (head + 1) * 2 * HS)
+            kv_out[pl.ds(low, TILE), key] = unit_rows(projected[:, key]).astype(jnp.bfloat16)
+            kv_out[pl.ds(low, TILE), value] = projected[:, value].astype(jnp.bfloat16)
+
+    for turn in range(1, PLANE):
+        for kind in range(2):
+            swap(kind, turn).wait_send()
+        send_tokens(turn).wait_send()
+        half_over(turn).wait_send()
+
+    @pl.loop(0, depth)
+    def _(turn):
+        for to in range(1, PLANE):
+            plane_out(turn, to).wait_send()
+        mixed_over(turn, core).wait_send()
+
+    @pl.loop(0, depth * PLANE)
+    def _(index):
+        @pl.when((z < depth - 1) & (index // PLANE <= z))
+        def _():
+            for kind in range(2):
+                pass_right(kind, index).wait_send()
+
+        @pl.when((z > 0) & (index // PLANE >= z))
+        def _():
+            for kind in range(2):
+                pass_left(kind, index).wait_send()
+
+
+def patch_block(
+    patch, mlp_gain, up, down, kv_gain, kv_weight, byte_states, query_weight, depth
+):
+    rows, features = patch.shape
+    thin = up.shape[0]
+    units = up.shape[1] // PLANE
+    wide = features // (2 * depth)
+    vmem = pl.BlockSpec(memory_space=pltpu.VMEM)
+    bf16 = lambda *shape: pltpu.VMEM(shape, jnp.bfloat16)
+    dma = lambda *shape: pltpu.SemaphoreType.DMA(shape)
+    return pl.pallas_call(
+        block_kernel,
+        in_specs=[vmem] * 8,
+        out_specs=[vmem] * 2,
+        out_shape=[
+            jax.ShapeDtypeStruct((rows, kv_weight.shape[1]), jnp.bfloat16),
+            jax.ShapeDtypeStruct((byte_states.shape[0], query_weight.shape[1]), jnp.bfloat16),
+        ],
+        scratch_shapes=[
+            bf16(features, units),
+            bf16(depth * PLANE, units, thin),
+            bf16(PLANE * rows, features),
+            bf16(PLANE * rows, units),
+            bf16(PLANE * rows, wide),
+            bf16(depth, PLANE * rows, wide),
+            bf16(PLANE * rows, wide),
+            bf16(depth, PLANE * rows, wide),
+            bf16(depth, PLANE, rows, wide),
+            bf16(2 * depth, rows, wide),
+            dma(2, PLANE), dma(2, PLANE), dma(2, depth * PLANE),
+            dma(2, depth * PLANE), dma(2, depth * PLANE),
+            dma(PLANE), dma(PLANE), dma(PLANE), dma(PLANE),
+            dma(2, depth), dma(depth, PLANE), dma(depth, PLANE), dma(depth), dma(depth), dma(2),
+        ],
+        compiler_params=pltpu.CompilerParams(
+            collective_id=0, has_side_effects=True, vmem_limit_bytes=62 * 2**20
+        ),
+        cost_estimate=pl.CostEstimate(
+            flops=40 * 10**9, bytes_accessed=60 * 10**6, transcendentals=0
+        ),
+    )(patch, mlp_gain[None], up, down, kv_gain[None], kv_weight, byte_states, query_weight)
 
 
 def attend_kernel(heads, distances, start, finish, scalars, ends, query, byte_patch, *refs):
@@ -141,6 +521,60 @@
     )(*operands)
 
 
+def patch_block_plain(
+    patch_states, mlp_gain, up_weight, down_weight, kv_gain, kv_weight, byte_states, query_weight
+):
+    seq = lax.axis_size("seq")
+    patch_rows = patch_states.shape[0]
+    size = PLANE if seq % PLANE == 0 else 1
+    groups = [[base + i for i in range(size)] for base in range(0, seq, size)]
+    across = [[base + i for base in range(0, seq, size)] for i in range(size)]
+    place = lax.rem(lax.axis_index("seq"), size)
+
+    up_part = lax.all_to_all(up_weight, "seq", 1, 0, axis_index_groups=groups, tiled=True)
+    down_part = lax.all_to_all(down_weight, "seq", 0, 1, axis_index_groups=groups, tiled=True)
+    up_all = lax.all_gather(up_part, "seq", axis=0, tiled=True, axis_index_groups=across)
+    down_all = lax.all_gather(down_part, "seq", axis=1, tiled=True, axis_index_groups=across)
+
+    normed = scale_rows(patch_states.astype(jnp.float32), mlp_gain.astype(jnp.float32)).astype(
+        jnp.bfloat16
+    )
+    tokens = lax.all_gather(normed, "seq", axis=0, tiled=True, axis_index_groups=groups)
+    heads_here = kv_weight.shape[1] // (2 * HS)
+    bytes_here = byte_states.shape[0]
+    query_proj = jnp.dot(byte_states, query_weight, preferred_element_type=jnp.float32).reshape(
+        bytes_here, heads_here, HS
+    )
+    queries = unit_rows(query_proj).astype(jnp.bfloat16).reshape(bytes_here, heads_here * HS)
+
+    preact = jnp.dot(tokens, up_all, preferred_element_type=jnp.float32)
+    hidden = jax.nn.gelu(preact, approximate=False).astype(jnp.bfloat16)
+    partial_value = jnp.dot(hidden, down_all, preferred_element_type=jnp.float32).astype(
+        jnp.bfloat16
+    )
+    part = sum_over_cores(partial_value, 1).astype(jnp.bfloat16)
+    part = part.reshape(size, patch_rows, part.shape[1])
+    mixed = lax.dynamic_index_in_dim(part, place, 0, keepdims=False).astype(jnp.float32)
+    for turn in range(1, size):
+        pairs = [(base + i, base + (i ^ turn)) for base in range(0, seq, size) for i in range(size)]
+        piece = lax.dynamic_index_in_dim(part, lax.bitwise_xor(place, turn), 0, keepdims=False)
+        mixed = mixed + lax.ppermute(piece, "seq", pairs).astype(jnp.float32)
+    mixed = join_cores(mixed.astype(jnp.bfloat16), 1).astype(jnp.float32)
+
+    kv_in = scale_rows(
+        patch_states.astype(jnp.float32) + mixed, kv_gain.astype(jnp.float32)
+    ).astype(jnp.bfloat16)
+    projected = jnp.dot(kv_in, kv_weight, preferred_element_type=jnp.float32).reshape(
+        patch_rows, heads_here, 2, HS
+    )
+    kv_pack = (
+        jnp.stack([unit_rows(projected[:, :, 0]), projected[:, :, 1]], axis=2)
+        .astype(jnp.bfloat16)
+        .reshape(patch_rows, heads_here * 2 * HS)
+    )
+    return kv_pack, queries
+
+
 def on_device(
     patch_states,
     mlp_gain,
@@ -157,54 +591,16 @@
     seq = lax.axis_size("seq")
     me = lax.axis_index("seq")
     patch_rows, features = patch_states.shape
-    size = 4 if seq % 4 == 0 else 1
-    groups = [[base + i for i in range(size)] for base in range(0, seq, size)]
-    across = [[base + i for base in range(0, seq, size)] for i in range(size)]
-    place = lax.rem(me, size)
-
-    up_part = lax.all_to_all(up_weight, "seq", 1, 0, axis_index_groups=groups, tiled=True)
-    down_part = lax.all_to_all(down_weight, "seq", 0, 1, axis_index_groups=groups, tiled=True)
-    up_all = lax.all_gather(up_part, "seq", axis=0, tiled=True, axis_index_groups=across)
-    down_all = lax.all_gather(down_part, "seq", axis=1, tiled=True, axis_index_groups=across)
-
-    normed = scale_rows(patch_states.astype(jnp.float32), mlp_gain.astype(jnp.float32)).astype(
-        jnp.bfloat16
-    )
-    tokens = lax.all_gather(normed, "seq", axis=0, tiled=True, axis_index_groups=groups)
-    counts = lax.all_gather(patch_counts, "seq", axis=0, tiled=True)
-
-    heads_here = kv_weight.shape[1] // (2 * HS)
     bytes_here = byte_states.shape[0]
-    query_proj = jnp.dot(byte_states, query_weight, preferred_element_type=jnp.float32).reshape(
-        bytes_here, heads_here, HS
-    )
-    queries = unit_rows(query_proj).astype(jnp.bfloat16).reshape(bytes_here, heads_here * HS)
-
-    preact = jnp.dot(tokens, up_all, preferred_element_type=jnp.float32)
-    hidden = jax.nn.gelu(preact, approximate=False).astype(jnp.bfloat16)
-    partial_value = jnp.dot(hidden, down_all, preferred_element_type=jnp.float32).astype(
-        jnp.bfloat16
-    )
-    part = sum_over_cores(partial_value, 1).astype(jnp.bfloat16)
-    part = part.reshape(size, patch_rows, part.shape[1])
-    mixed = lax.dynamic_index_in_dim(part, place, 0, keepdims=False).astype(jnp.float32)
-    for turn in range(1, size):
-        pairs = [(base + i, base + (i ^ turn)) for base in range(0, seq, size) for i in range(size)]
-        piece = lax.dynamic_index_in_dim(part, lax.bitwise_xor(place, turn), 0, keepdims=False)
-        mixed = mixed + lax.ppermute(piece, "seq", pairs).astype(jnp.float32)
-    mixed = join_cores(mixed.astype(jnp.bfloat16), 1).astype(jnp.float32)
-
-    kv_in = scale_rows(
-        patch_states.astype(jnp.float32) + mixed, kv_gain.astype(jnp.float32)
-    ).astype(jnp.bfloat16)
-    projected = jnp.dot(kv_in, kv_weight, preferred_element_type=jnp.float32).reshape(
-        patch_rows, heads_here, 2, HS
-    )
-    kv_pack = (
-        jnp.stack([unit_rows(projected[:, :, 0]), projected[:, :, 1]], axis=2)
-        .astype(jnp.bfloat16)
-        .reshape(patch_rows, heads_here * 2 * HS)
-    )
+    operands = (
+        patch_states, mlp_gain, up_weight, down_weight, kv_gain, kv_weight, byte_states,
+        query_weight,
+    )
+    fits = seq == 4 * PLANE and lax.axis_size("mp") == 2 and up_weight.shape[0] % 128 == 0
+    if fits and up_weight.shape[1] % (PLANE * 128) == 0:
+        kv_pack, queries = patch_block(*operands, seq // PLANE)
+    else:
+        kv_pack, queries = patch_block_plain(*operands)
 
     fewest = patch_rows // 2
     depth = (WIN + fewest - 2) // fewest
@@ -220,7 +616,7 @@
         blocks.append(
             lax.ppermute(source, "seq", [(i, i + back) for i in range(max(0, seq - back))])
         )
-        held = jnp.where(me >= back, counts[jnp.maximum(me - back, 0)], 0)
+        held = lax.ppermute(own_count, "seq", [(i, i + back) for i in range(max(0, seq - back))])
         first = first - held
         if need <= fewest:
             scalars += [first + held - need, jnp.where(me >= back, need, 0)]

time: 553 us -> 328 us (0.59)
  the two profiles are of different devices: /device:TPU:9 before, /device:TPU:29 now
where the time goes in v2:
time: 328 us
  Pallas kernels  206 us (63%)
  waiting for transfers between devices  90.2 us (28%)
  local copies, waits for them, and re-layouts  14.8 us (5%)
  starting transfers between devices  11.8 us (4%)
    pallas_call x1, Pallas kernels, patch_block(): pl.pallas_call(block_kernel, in_specs=[vmem] * 8, out_specs=[vmem] * 2, o...  171 us
    ppermute x3, waiting for transfers between devices, on_device(): lax.ppermute(own_count, 'seq', [(i, i + back) for i in range(max(0, seq -...  87.8 us
    pallas_call x5, Pallas kernels, attend(): pl.pallas_call(functools.partial(attend_kernel, heads, distances, start,...  35.1 us
    unnamed x18, local copies, waits for them, and re-layouts  7.81 us
  transfers between devices with their start and end apart: 8, of which 3 were waited for; matrix products, arithmetic and copies ran while one was open for 1% of the time, Pallas kernels for 9%

profile of v2, /device:TPU:29, one launch (start us, length us, event | category | flops | bytes accessed | tf_op | source)
XLA Modules:
  0.0 327.8 jit_solution(14038978898105113864)
XLA Ops:
  0.0 1.3 broadcast_in_dim.10.kv_gain
  1.3 1.3 broadcast_in_dim.9.mlp_gain
  2.6 0.0 copy-start.8
  2.6 170.6 %shard_map.109 = (bf16[512,1024]{1,0:T(8,128)(2,1)}, bf16[1024,512]{1,0:T(8,128)(2,1)}) custom-call(bf16[512,2048]{1,0:T(8,128)(2,1)} %patch.1, bf16[1,2048]{1,0:T(2,128)(2,1)} %broadcast_in_dim.9.mlp_gain, bf16[128,3584]{1,0:T(8,128)(2,1)} %up.1, bf16[3584,128]{1,0:T(8,128)(2,1)} %down.1, bf16[1,2048]{1,0:T(2,128)(2,1)} %broadcast_in_dim.10.kv_gain, ...), custom_call_target="tpu_custom_call" | custom-call | flops 40000000000 | bytes 60000000 | tf_op jit(solution)/shard_map/pallas_call | solution.py:396
  173.2 2.3 collective-permute-start.6
  175.4 1.3 collective-permute-start.5
  176.7 1.9 collective-permute-start
  178.7 1.3 collective-permute-start.1
  180.0 1.3 collective-permute-start.4
  181.9 0.0 copy-done.8
  181.9 0.1 fusion
  182.0 0.1 pad_add_fusion
  182.1 0.1 reshape.7.ends
  182.2 0.2 copy.16.byte_patch
  182.4 2.0 constant_dynamic-slice_fusion.1
  184.4 39.3 %collective-permute-done = s32[]{:T(128)} collective-permute-done((s32[]{:T(128)}, s32[]{:T(128)}, u32[]{:S(2)}, u32[]{:S(2)}) %collective-permute-start) | collective-permute-done | bytes 36 | tf_op jit(solution)/shard_map/ppermute | solution.py:619
  223.7 1.3 collective-permute-start.2
  225.6 0.0 collective-permute-done.1
  225.7 1.5 collective-permute-start.3
  227.8 48.5 %collective-permute-done.2 = s32[]{:T(128)} collective-permute-done((s32[]{:T(128)}, s32[]{:T(128)}, u32[]{:S(2)}, u32[]{:S(2)}) %collective-permute-start.2) | collective-permute-done | bytes 36 | tf_op jit(solution)/shard_map/ppermute | solution.py:619
  276.9 2.0 stack.38.scalars
  278.8 0.0 copy-start.2
  278.8 1.2 copy-done.2
  280.0 0.0 copy-start.4
  280.0 1.2 copy-done.4
  281.3 0.0 copy-start.3
  281.3 5.2 %shard_map.110 = (f32[1024,512]{1,0:T(8,128)S(1)}, f32[1024,512]{1,0:T(8,128)}) custom-call(s32[10]{0:T(128)S(1)} %stack.38.scalars, s32[8]{0:T(128)S(1)} %reshape.7.ends, bf16[1024,512]{1,0:T(8,128)(2,1)S(1)} %copy-done.2, s32[1024,1]{1,0:T(8,128)S(1)} %copy.16.byte_patch, bf16[512,1024]{1,0:T(8,128)(2,1)S(1)} %copy-done.4), custom_call_target="tpu_custom_call" | custom-call | flops 2147483648 | bytes 1048576 | tf_op jit(solution)/shard_map/pallas_call | solution.py:510
  286.4 0.0 copy-start.7
  286.4 1.3 copy-done.7
  287.8 0.0 collective-permute-done.6.refs_0_
  287.8 0.0 copy-done.3
  287.8 8.3 %shard_map.111 = (f32[1024,512]{1,0:T(8,128)S(1)}, f32[1024,512]{1,0:T(8,128)}) custom-call(s32[10]{0:T(128)S(1)} %stack.38.scalars, s32[8]{0:T(128)S(1)} %reshape.7.ends, bf16[1024,512]{1,0:T(8,128)(2,1)S(1)} %copy-done.3, s32[1024,1]{1,0:T(8,128)S(1)} %copy.16.byte_patch, bf16[512,1024]{1,0:T(8,128)(2,1)} %collective-permute-done.6.refs_0_, ...), custom_call_target="tpu_custom_call" | custom-call | flops 2147483648 | bytes 1048576 | tf_op jit(solution)/shard_map/pallas_call | solution.py:510
  296.1 0.0 copy-start.6
  296.1 1.3 copy-done.6
  297.5 0.0 collective-permute-done.5.refs_0_
  297.5 7.9 %shard_map.112 = (f32[1024,512]{1,0:T(8,128)S(1)}, f32[1024,512]{1,0:T(8,128)}) custom-call(s32[10]{0:T(128)S(1)} %stack.38.scalars, s32[8]{0:T(128)S(1)} %reshape.7.ends, bf16[1024,512]{1,0:T(8,128)(2,1)S(1)} %copy-done.3, s32[1024,1]{1,0:T(8,128)S(1)} %copy.16.byte_patch, bf16[512,1024]{1,0:T(8,128)(2,1)S(1)} %collective-permute-done.5.refs_0_, ...), custom_call_target="tpu_custom_call" | custom-call | flops 2147483648 | bytes 1048576 | tf_op jit(solution)/shard_map/pallas_call | solution.py:510
  305.4 0.0 copy-start.5
  305.4 1.3 copy-done.5
  306.7 0.0 collective-permute-done.4.refs_0_
  306.8 0.0 copy-start.1
  306.8 8.0 %shard_map.113 = (f32[1024,512]{1,0:T(8,128)S(1)}, f32[1024,512]{1,0:T(8,128)}) custom-call(s32[10]{0:T(128)S(1)} %stack.38.scalars, s32[8]{0:T(128)S(1)} %reshape.7.ends, bf16[1024,512]{1,0:T(8,128)(2,1)S(1)} %copy-done.3, s32[1024,1]{1,0:T(8,128)S(1)} %copy.16.byte_patch, bf16[512,1024]{1,0:T(8,128)(2,1)S(1)} %collective-permute-done.4.refs_0_, ...), custom_call_target="tpu_custom_call" | custom-call | flops 2147483648 | bytes 1048576 | tf_op jit(solution)/shard_map/pallas_call | solution.py:510
  314.8 0.0 copy-start
  314.8 1.3 copy-done
  316.1 0.0 collective-permute-done.3.refs_0_
  316.1 0.0 copy-done.1
  316.1 5.6 %shard_map.114 = bf16[1024,1024]{1,0:T(8,128)(2,1)S(1)} custom-call(s32[10]{0:T(128)S(1)} %stack.38.scalars, s32[8]{0:T(128)S(1)} %reshape.7.ends, bf16[1024,512]{1,0:T(8,128)(2,1)S(1)} %copy-done.3, s32[1024,1]{1,0:T(8,128)S(1)} %copy.16.byte_patch, bf16[256,1024]{1,0:T(8,128)(2,1)S(1)} %collective-permute-done.3.refs_0_, f32[1024,512]{1,0:T(8,128)} %copy-done, ...), custom_call_target="tpu_custom_call" | custom-call | flops 1073741824 | bytes 524288 | tf_op jit(solution)/shard_map/pallas_call | solution.py:510
  321.7 0.1 constant_dynamic-slice_fusion
  321.8 1.0 collective-permute-start.7
  322.8 2.4 collective-permute-done.7
  325.2 2.6 add_convert_fusion
  (1 shorter events, 0.0 us)
Async XLA Ops:
  2.6 179.3 %copy-start.8 = (s32[1024]{0:T(1024)S(1)}, s32[1024]{0:T(1024)}, u32[]{:S(2)}) copy-start(s32[1024]{0:T(1024)} %param.21) | copy-start | bytes 12292
  173.2 114.6 %collective-permute-start.6 = (bf16[512,1024]{1,0:T(8,128)(2,1)}, bf16[512,1024]{1,0:T(8,128)(2,1)}, u32[]{:S(2)}, u32[]{:S(2)}) collective-permute-start(bf16[512,1024]{1,0:T(8,128)(2,1)} %get-tuple-element.16.refs_0_), channel_id=1, source_target_pairs={{0,2},{2,4},{4,6},{6,8},{8,10},{10,12},{12,14},{14,16},{16,18},{18... | collective-permute-start | bytes 3145736 | tf_op jit(solution)/shard_map/ppermute | solution.py:617
  175.4 122.1 %collective-permute-start.5 = (bf16[512,1024]{1,0:T(8,128)(2,1)}, bf16[512,1024]{1,0:T(8,128)(2,1)S(1)}, u32[]{:S(2)}, u32[]{:S(2)}) collective-permute-start(bf16[512,1024]{1,0:T(8,128)(2,1)} %get-tuple-element.16.refs_0_), channel_id=1, source_target_pairs={{0,4},{2,6},{4,8},{6,10},{8,12},{10,14},{12,16},{14,18},{16,20},{1... | collective-permute-start | bytes 3145736 | tf_op jit(solution)/shard_map/ppermute | solution.py:617
  176.7 47.0 %collective-permute-start = (s32[]{:T(128)}, s32[]{:T(128)}, u32[]{:S(2)}, u32[]{:S(2)}) collective-permute-start(s32[]{:T(128)} %bitcast), channel_id=1, source_target_pairs={{0,2},{2,4},{4,6},{6,8},{8,10},{10,12},{12,14},{14,16},{16,18},{18... | collective-permute-start | bytes 20 | tf_op jit(solution)/shard_map/ppermute | solution.py:619
  178.7 47.0 %collective-permute-start.1 = (s32[]{:T(128)}, s32[]{:T(128)}, u32[]{:S(2)}, u32[]{:S(2)}) collective-permute-start(s32[]{:T(128)} %bitcast), channel_id=1, source_target_pairs={{0,4},{2,6},{4,8},{6,10},{8,12},{10,14},{12,16},{14,18},{16,20},{1... | collective-permute-start | bytes 20 | tf_op jit(solution)/shard_map/ppermute | solution.py:619
  180.0 126.8 %collective-permute-start.4 = (bf16[512,1024]{1,0:T(8,128)(2,1)}, bf16[512,1024]{1,0:T(8,128)(2,1)S(1)}, u32[]{:S(2)}, u32[]{:S(2)}) collective-permute-start(bf16[512,1024]{1,0:T(8,128)(2,1)} %get-tuple-element.16.refs_0_), channel_id=1, source_target_pairs={{0,6},{2,8},{4,10},{6,12},{8,14},{10,16},{12,18},{14,20},{16,22},{... | collective-permute-start | bytes 3145736 | tf_op jit(solution)/shard_map/ppermute | solution.py:617
  223.7 52.5 %collective-permute-start.2 = (s32[]{:T(128)}, s32[]{:T(128)}, u32[]{:S(2)}, u32[]{:S(2)}) collective-permute-start(s32[]{:T(128)} %bitcast), channel_id=1, source_target_pairs={{0,6},{2,8},{4,10},{6,12},{8,14},{10,16},{12,18},{14,20},{16,22},{... | collective-permute-start | bytes 20 | tf_op jit(solution)/shard_map/ppermute | solution.py:619
  225.7 90.5 %collective-permute-start.3 = (bf16[256,1024]{1,0:T(8,128)(2,1)}, bf16[256,1024]{1,0:T(8,128)(2,1)S(1)}, u32[]{:S(2)}, u32[]{:S(2)}) collective-permute-start(bf16[256,1024]{1,0:T(8,128)(2,1)} %constant_dynamic-slice_fusion.1), channel_id=1, source_target_pairs={{0,8},{2,10},{4,12},{6,14},{8,16},{10,18},{12,20},{14,22},{16,24},... | collective-permute-start | bytes 1572872 | tf_op jit(solution)/shard_map/ppermute | solution.py:617
  278.8 1.2 copy-start.2
  280.0 1.2 copy-start.4
  281.3 6.5 %copy-start.3 = (bf16[1024,512]{1,0:T(8,128)(2,1)S(1)}, bf16[1024,512]{1,0:T(8,128)(2,1)}, u32[]{:S(2)}) copy-start(bf16[1024,512]{1,0:T(8,128)(2,1)} %get-tuple-element.15.query) | copy-start | bytes 3145732
  286.4 1.3 copy-start.7
  296.1 1.3 copy-start.6
  305.4 1.3 copy-start.5
  306.8 9.4 %copy-start.1 = (bf16[512,1024]{1,0:T(8,128)(2,1)S(1)}, bf16[512,1024]{1,0:T(8,128)(2,1)}, u32[]{:S(2)}) copy-start(bf16[512,1024]{1,0:T(8,128)(2,1)} %refs_3_.1) | copy-start | bytes 3145732
  314.8 1.3 copy-start
  321.8 3.4 %collective-permute-start.7 = (bf16[512,1024]{1,0:T(8,128)(2,1)S(1)}, bf16[512,1024]{1,0:T(8,128)(2,1)}, u32[]{:S(2)}, u32[]{:S(2)}) collective-permute-start(bf16[512,1024]{1,0:T(8,128)(2,1)S(1)} %constant_dynamic-slice_fusion), channel_id=1, source_target_pairs={{0,1},{1,0},{2,3},{3,2},{4,5},{5,4},{6,7},{7,6},{8,9},{9,8},{10,11... | collective-permute-start | bytes 3145736 | tf_op jit(solution)/shard_map/ppermute | solution.py:36

commit v3 on v2

--- a/solution.py
+++ b/solution.py
@@ -49,12 +49,13 @@
 
 
 def block_kernel(
-    patch, mlp_gain, up, down, kv_gain, kv_weight, byte_states, query_weight,
-    kv_out, query_out,
+    patch, mlp_gain, up, down, kv_gain, kv_weight, byte_states, query_weight, count,
+    kv_out, query_out, count_out,
     up_all, down_all, tokens, hidden, core_send, core_got, kept, plane_send, plane_got, mixed,
     swap_send, swap_recv, chunk_recv, right_send, left_send,
     token_send, token_recv, half_send, half_recv,
     core_sems, plane_sems, plane_recv, mixed_send, mixed_recv, local_sems,
+    halo_send, halo_recv, count_send, count_recv,
 ):
     seq, core = lax.axis_index("seq"), lax.axis_index("mp")
     depth = lax.axis_size("seq") // PLANE
@@ -176,6 +177,69 @@
     own[0].wait()
     spread(0, seq)
 
+    def later(turn):
+        return member(turn) > place
+
+    def source(turn):
+        return jnp.where(later(turn), 0, PLANE)
+
+    def distance(turn):
+        return lax.rem(member(turn) - place + PLANE, PLANE)
+
+    def from_distance(turn):
+        return lax.rem(place - member(turn) + PLANE, PLANE)
+
+    def count_on():
+        return remote(
+            count_out.at[0], count_out.at[PLANE], count_send.at[0], count_recv.at[0],
+            (seq + PLANE, core),
+        )
+
+    def count_over(turn):
+        return remote(
+            count_out.at[source(turn)], count_out.at[distance(turn)], count_send.at[turn],
+            count_recv.at[turn], peer(turn),
+        )
+
+    def count_arrives(turn):
+        part = count_out.at[from_distance(turn)]
+        return remote(part, part, count_send.at[turn], count_recv.at[turn], peer(turn))
+
+    def count_chain():
+        @pl.when(z > 0)
+        def _():
+            count_on().wait_recv()
+
+        for turn in range(1, PLANE):
+            @pl.when(later(turn) | (z > 0))
+            def _(turn=turn):
+                count_over(turn).start()
+
+    count_out[0] = count[...]
+
+    @pl.when(z < depth - 1)
+    def _():
+        count_on().start()
+
+    def piece(step):
+        return pl.ds(pl.multiple_of(step * TILE, TILE), TILE)
+
+    def halo_on(step):
+        return remote(
+            kv_out.at[0, piece(step), :], kv_out.at[PLANE, piece(step), :],
+            halo_send.at[0, step], halo_recv.at[0, step], (seq + PLANE, core),
+        )
+
+    def halo_over(turn, step):
+        return remote(
+            kv_out.at[source(turn), piece(step), :], kv_out.at[distance(turn), piece(step), :],
+            halo_send.at[turn, step], halo_recv.at[turn, step], peer(turn),
+        )
+
+    def halo_arrives(turn, step):
+        part = kv_out.at[from_distance(turn), piece(step), :]
+        return remote(part, part, halo_send.at[turn, step], halo_recv.at[turn, step], peer(turn))
+
     gain = mlp_gain[...].astype(jnp.float32)
     row_start = pl.multiple_of(place * rows, rows)
 
@@ -235,6 +299,7 @@
             )
         hop(0, step)
 
+    count_chain()
     own[1].wait()
     spread(1, seq)
     for turn in range(1, PLANE):
@@ -355,8 +420,53 @@
         for head in range(heads):
             key = slice(head * 2 * HS, head * 2 * HS + HS)
             value = slice(head * 2 * HS + HS, (head + 1) * 2 * HS)
-            kv_out[pl.ds(low, TILE), key] = unit_rows(projected[:, key]).astype(jnp.bfloat16)
-            kv_out[pl.ds(low, TILE), value] = projected[:, value].astype(jnp.bfloat16)
+            kv_out[0, pl.ds(low, TILE), key] = unit_rows(projected[:, key]).astype(jnp.bfloat16)
+            kv_out[0, pl.ds(low, TILE), value] = projected[:, value].astype(jnp.bfloat16)
+
+        @pl.when(z < depth - 1)
+        def _():
+            halo_on(tile).start()
+
+        for turn in range(1, PLANE):
+            @pl.when(later(turn))
+            def _(turn=turn):
+                halo_over(turn, tile).start()
+
+    @pl.when(z > 0)
+    def _():
+        @pl.loop(0, rows // TILE)
+        def _(step):
+            halo_on(step).wait_recv()
+            for turn in range(1, PLANE):
+                @pl.when(member(turn) < place)
+                def _(turn=turn):
+                    halo_over(turn, step).start()
+
+    for turn in range(1, PLANE):
+        @pl.when((member(turn) < place) | (z > 0))
+        def _(turn=turn):
+            count_arrives(turn).wait_recv()
+
+            @pl.loop(0, rows // TILE)
+            def _(step):
+                halo_arrives(turn, step).wait_recv()
+
+    for turn in range(1, PLANE):
+        @pl.when(later(turn) | (z > 0))
+        def _(turn=turn):
+            count_over(turn).wait_send()
+
+            @pl.loop(0, rows // TILE)
+            def _(step):
+                halo_over(turn, step).wait_send()
+
+    @pl.when(z < depth - 1)
+    def _():
+        count_on().wait_send()
+
+        @pl.loop(0, rows // TILE)
+        def _(step):
+            halo_on(step).wait_send()
 
     for turn in range(1, PLANE):
         for kind in range(2):
@@ -384,7 +494,7 @@
 
 
 def patch_block(
-    patch, mlp_gain, up, down, kv_gain, kv_weight, byte_states, query_weight, depth
+    patch, mlp_gain, up, down, kv_gain, kv_weight, byte_states, query_weight, count, depth
 ):
     rows, features = patch.shape
     thin = up.shape[0]
@@ -395,11 +505,12 @@
     dma = lambda *shape: pltpu.SemaphoreType.DMA(shape)
     return pl.pallas_call(
         block_kernel,
-        in_specs=[vmem] * 8,
-        out_specs=[vmem] * 2,
+        in_specs=[vmem] * 9,
+        out_specs=[vmem] * 3,
         out_shape=[
-            jax.ShapeDtypeStruct((rows, kv_weight.shape[1]), jnp.bfloat16),
+            jax.ShapeDtypeStruct((PLANE + 1, rows, kv_weight.shape[1]), jnp.bfloat16),
             jax.ShapeDtypeStruct((byte_states.shape[0], query_weight.shape[1]), jnp.bfloat16),
+            jax.ShapeDtypeStruct((PLANE + 1, 8, 128), jnp.int32),
         ],
         scratch_shapes=[
             bf16(features, units),
@@ -416,6 +527,7 @@
             dma(2, depth * PLANE), dma(2, depth * PLANE),
             dma(PLANE), dma(PLANE), dma(PLANE), dma(PLANE),
             dma(2, depth), dma(depth, PLANE), dma(depth, PLANE), dma(depth), dma(depth), dma(2),
+            dma(PLANE, rows // TILE), dma(PLANE, rows // TILE), dma(PLANE), dma(PLANE),
         ],
         compiler_params=pltpu.CompilerParams(
             collective_id=0, has_side_effects=True, vmem_limit_bytes=62 * 2**20
@@ -423,102 +535,83 @@
         cost_estimate=pl.CostEstimate(
             flops=40 * 10**9, bytes_accessed=60 * 10**6, transcendentals=0
         ),
-    )(patch, mlp_gain[None], up, down, kv_gain[None], kv_weight, byte_states, query_weight)
-
-
-def attend_kernel(heads, distances, start, finish, scalars, ends, query, byte_patch, *refs):
-    kv_refs, refs = refs[: len(distances)], refs[len(distances) :]
-    if not start:
-        (num_in, den_in), refs = refs[:2], refs[2:]
-    if finish:
-        out_weight, out, num, den = refs
-    else:
-        num, den = refs
-    if start:
-        num[...] = jnp.zeros_like(num)
-        den[...] = jnp.zeros_like(den)
-    else:
-        num[...] = num_in[...]
-        den[...] = den_in[...]
+    )(
+        patch, mlp_gain[None], up, down, kv_gain[None], kv_weight, byte_states, query_weight,
+        jnp.broadcast_to(count, (8, 128)),
+    )
+
+
+def attend_kernel(
+    heads, blocks, counts, by_byte, query, byte_patch, kv, out_weight, out, num, den
+):
+    num[...] = jnp.zeros_like(num)
+    den[...] = jnp.zeros_like(den)
+    me = lax.axis_index("seq")
+    rows = query.shape[0]
     tile = pl.program_id(0)
-    lowest, highest = ends[2 * tile], ends[2 * tile + 1]
+    lowest, highest = by_byte[tile * rows], by_byte[tile * rows + rows - 1]
     scale = 2.0 / math.sqrt(HS) * math.log2(math.e)
-    for distance, kv_ref in zip(distances, kv_refs):
-        first, live = scalars[2 * distance], scalars[2 * distance + 1]
-        for low in range(0, kv_ref.shape[0], KEY_TILE):
+    slots = kv.shape[0] // blocks
+    first = jnp.int32(0)
+    for back in range(blocks):
+        live = jnp.where(me >= back, counts[back], 0)
+        if back:
+            first = first - live
+        for low in range(0, slots, KEY_TILE):
             last = first + jnp.minimum(live, low + KEY_TILE) - 1
             seen = (low < live) & (first + low <= highest) & (last > lowest - WIN)
 
             @pl.when(seen)
-            def _(kv_ref=kv_ref, low=low, first=first, live=live):
-                rows = query.shape[0]
+            def _(start=back * slots + low, low=low, first=first, live=live):
                 position = low + lax.broadcasted_iota(jnp.int32, (rows, KEY_TILE), 1)
                 gap = byte_patch[...] - first - position
                 usable = (position < live) & (gap >= 0) & (gap < WIN)
+                keys = slice(start, start + KEY_TILE)
                 for head in range(heads):
                     columns = slice(head * HS, (head + 1) * HS)
-                    key = kv_ref[low : low + KEY_TILE, head * 2 * HS : head * 2 * HS + HS]
-                    value = kv_ref[low : low + KEY_TILE, head * 2 * HS + HS : (head + 1) * 2 * HS]
                     scores = lax.dot_general(
                         query[:, columns],
-                        key,
+                        kv[keys, head * 2 * HS : head * 2 * HS + HS],
                         (((1,), (1,)), ((), ())),
                         preferred_element_type=jnp.float32,
                     )
                     weights = jnp.where(usable, jnp.exp2(scores * scale), 0.0)
                     den[:, columns] += weights[:, :HS] + weights[:, HS:]
                     num[:, columns] += jnp.dot(
-                        weights.astype(jnp.bfloat16), value, preferred_element_type=jnp.float32
+                        weights.astype(jnp.bfloat16),
+                        kv[keys, head * 2 * HS + HS : (head + 1) * 2 * HS],
+                        preferred_element_type=jnp.float32,
                     )
 
-    if finish:
-        parts = []
-        for head in range(heads):
-            columns = slice(head * HS, (head + 1) * HS)
-            total = jnp.sum(den[:, columns], axis=1, keepdims=True)
-            parts.append((num[:, columns] / total).astype(jnp.bfloat16))
-        attended = jnp.concatenate(parts, axis=1)
-        out[...] = jnp.dot(
-            attended, out_weight[...], preferred_element_type=jnp.float32
-        ).astype(jnp.bfloat16)
-
-
-def attend(distances, scalars, ends, query, byte_patch, blocks, sums=None, out_weight=None):
+    parts = []
+    for head in range(heads):
+        columns = slice(head * HS, (head + 1) * HS)
+        total = jnp.sum(den[:, columns], axis=1, keepdims=True)
+        parts.append((num[:, columns] / total).astype(jnp.bfloat16))
+    out[...] = jnp.dot(
+        jnp.concatenate(parts, axis=1), out_weight[...], preferred_element_type=jnp.float32
+    ).astype(jnp.bfloat16)
+
+
+def attend(query, byte_patch, counts, kv, out_weight):
     rows, width = query.shape
-    heads = width // HS
-    tile = rows // (ends.shape[0] // 2)
-    start, finish = sums is None, out_weight is not None
+    tile = min(256, rows)
+    blocks = counts.shape[0]
     smem = pl.BlockSpec(memory_space=pltpu.SMEM)
     tiled = lambda columns: pl.BlockSpec((tile, columns), lambda i: (i, 0))
     whole = lambda array: pl.BlockSpec(array.shape, lambda i: (0, 0))
-    operands = [scalars, ends, query, byte_patch, *blocks]
-    in_specs = [smem, smem, tiled(width), tiled(1)] + [whole(block) for block in blocks]
-    if not start:
-        operands += list(sums)
-        in_specs += [tiled(width), tiled(width)]
-    if finish:
-        operands.append(out_weight)
-        in_specs.append(whole(out_weight))
-        out_shape = jax.ShapeDtypeStruct((rows, out_weight.shape[1]), jnp.bfloat16)
-        out_specs = tiled(out_weight.shape[1])
-        scratch = [pltpu.VMEM((tile, width), jnp.float32)] * 2
-    else:
-        out_shape = [jax.ShapeDtypeStruct((rows, width), jnp.float32)] * 2
-        out_specs = [tiled(width)] * 2
-        scratch = []
-    keys = sum(block.shape[0] for block in blocks)
     return pl.pallas_call(
-        functools.partial(attend_kernel, heads, distances, start, finish),
+        functools.partial(attend_kernel, width // HS, blocks),
         grid=(rows // tile,),
-        in_specs=in_specs,
-        out_specs=out_specs,
-        out_shape=out_shape,
-        scratch_shapes=scratch,
+        in_specs=[smem, smem, tiled(width), tiled(1), whole(kv), whole(out_weight)],
+        out_specs=tiled(out_weight.shape[1]),
+        out_shape=jax.ShapeDtypeStruct((rows, out_weight.shape[1]), jnp.bfloat16),
+        scratch_shapes=[pltpu.VMEM((tile, width), jnp.float32)] * 2,
         compiler_params=pltpu.CompilerParams(vmem_limit_bytes=48 * 2**20),
         cost_estimate=pl.CostEstimate(
-            flops=8 * rows * keys * width, bytes_accessed=4 * keys * width, transcendentals=0
+            flops=4 * rows * kv.shape[0] * width, bytes_accessed=4 * kv.size, transcendentals=0
         ),
-    )(*operands)
+    )(counts, byte_patch, query, byte_patch[:, None], kv, out_weight)
 
 
 def patch_block_plain(
@@ -589,48 +682,28 @@
     byte_patch,
 ):
     seq = lax.axis_size("seq")
-    me = lax.axis_index("seq")
-    patch_rows, features = patch_states.shape
-    bytes_here = byte_states.shape[0]
+    patch_rows = patch_states.shape[0]
     operands = (
         patch_states, mlp_gain, up_weight, down_weight, kv_gain, kv_weight, byte_states,
         query_weight,
     )
-    fits = seq == 4 * PLANE and lax.axis_size("mp") == 2 and up_weight.shape[0] % 128 == 0
-    if fits and up_weight.shape[1] % (PLANE * 128) == 0:
-        kv_pack, queries = patch_block(*operands, seq // PLANE)
+    fewest = patch_rows // 2
+    depth = (WIN + fewest - 2) // fewest
+    fits = seq == 4 * PLANE and lax.axis_size("mp") == 2 and depth == PLANE
+    fits = fits and up_weight.shape[0] % 128 == 0 and up_weight.shape[1] % (PLANE * 128) == 0
+    if fits:
+        kv_all, queries, counts = patch_block(*operands, patch_counts, seq // PLANE)
+        counts = counts[:, 0, 0]
     else:
         kv_pack, queries = patch_block_plain(*operands)
-
-    fewest = patch_rows // 2
-    depth = (WIN + fewest - 2) // fewest
-    own_count = patch_counts[0]
-    blocks = [kv_pack]
-    scalars = [jnp.zeros((), jnp.int32), own_count]
-    first = jnp.zeros((), jnp.int32)
-    for back in range(1, depth + 1):
-        need = min(patch_rows, -(-(WIN - 1 - (back - 1) * fewest) // KEY_TILE) * KEY_TILE)
-        source = kv_pack
-        if need <= fewest:
-            source = lax.dynamic_slice_in_dim(kv_pack, own_count - need, need, 0)
-        blocks.append(
-            lax.ppermute(source, "seq", [(i, i + back) for i in range(max(0, seq - back))])
-        )
-        held = lax.ppermute(own_count, "seq", [(i, i + back) for i in range(max(0, seq - back))])
-        first = first - held
-        if need <= fewest:
-            scalars += [first + held - need, jnp.where(me >= back, need, 0)]
-        else:
-            scalars += [first, held]
-    scalars = jnp.stack(scalars).astype(jnp.int32)
-    tile = min(256, bytes_here)
-    by_tile = byte_patch.reshape(bytes_here // tile, tile)
-    ends = jnp.stack([by_tile[:, 0], by_tile[:, -1]], axis=1).reshape(-1)
-    columns = byte_patch[:, None]
-    sums = attend((0,), scalars, ends, queries, columns, blocks[:1])
-    for back in range(1, depth):
-        sums = attend((back,), scalars, ends, queries, columns, blocks[back : back + 1], sums)
-    term = attend((depth,), scalars, ends, queries, columns, blocks[depth:], sums, out_weight)
+        kv_all, counts = [kv_pack], [patch_counts]
+        for back in range(1, depth + 1):
+            pairs = [(i, i + back) for i in range(max(0, seq - back))]
+            kv_all.append(lax.ppermute(kv_pack, "seq", pairs))
+            counts.append(lax.ppermute(patch_counts, "seq", pairs))
+        kv_all, counts = jnp.stack(kv_all), jnp.concatenate(counts)
+    kv_all = kv_all.reshape((depth + 1) * patch_rows, kv_all.shape[2])
+    term = attend(queries, byte_patch, counts, kv_all, out_weight)
     return sum_over_cores(term, 0).astype(jnp.bfloat16)
 
 

time: 328 us -> 260 us (0.79)
  the two profiles are of different devices: /device:TPU:29 before, /device:TPU:9 now
where the time goes in v3:
time: 260 us; the launch traced here: 258 us
  Pallas kernels  245 us (94%)
  local copies, waits for them, and re-layouts  6.84 us (3%)
    pallas_call x1, Pallas kernels, patch_block(): pl.pallas_call(block_kernel, in_specs=[vmem] * 9, out_specs=[vmem] * 3, o...  225 us
    pallas_call x1, Pallas kernels, attend(): pl.pallas_call(functools.partial(attend_kernel, width // HS, blocks), gri...  20.2 us
  transfers between devices with their start and end apart: 1, of which 1 were waited for; matrix products, arithmetic and copies ran while one was open for 0% of the time, Pallas kernels for 0%

profile of v3, /device:TPU:9, one launch (start us, length us, event | category | flops | bytes accessed | tf_op | source)
XLA Modules:
  0.0 258.5 jit_solution(3980804679604604649)
XLA Ops:
  0.0 1.3 broadcast_in_dim.14.mlp_gain
  1.3 1.3 broadcast_in_dim.15.kv_gain
  3.2 0.6 broadcast_in_dim.16.count
  3.8 0.0 copy-start
  3.8 224.8 %shard_map.112 = (bf16[5,512,1024]{2,1,0:T(8,128)(2,1)}, bf16[1024,512]{1,0:T(8,128)(2,1)}, s32[5,8,128]{2,1,0:T(8,128)}) custom-call(bf16[512,2048]{1,0:T(8,128)(2,1)} %patch.1, bf16[1,2048]{1,0:T(2,128)(2,1)} %broadcast_in_dim.14.mlp_gain, bf16[128,3584]{1,0:T(8,128)(2,1)} %up.1, bf16[3584,128]{1,0:T(8,128)(2,1)} %down.1, ...), custom_call_target="tpu_custom_call" | custom-call | flops 40000000000 | bytes 60000000 | tf_op jit(solution)/shard_map/pallas_call | solution.py:506
  228.7 0.9 slice_reduce_fusion.counts
  229.6 0.0 copy-done
  229.6 0.2 copy.12.byte_patch
  229.8 0.0 copy-start.1
  229.8 1.2 copy-done.1
  231.0 0.0 copy-start.2
  231.0 1.2 copy-done.2
  232.3 20.2 %shard_map.113 = bf16[1024,1024]{1,0:T(8,128)(2,1)S(1)} custom-call(s32[5]{0:T(128)S(1)} %slice_reduce_fusion.counts, s32[1024]{0:T(1024)S(1)} %copy-done, bf16[1024,512]{1,0:T(8,128)(2,1)S(1)} %copy-done.2, s32[1024,1]{1,0:T(8,128)S(1)} %copy.12.byte_patch, bf16[2560,1024]{1,0:T(8,128)(2,1)} %bitcast.5, bf16[512,1024]{1,0:T(8,128)(2,1)S(1)} %copy-done.1), custom_call_target="tpu_custom_call" | custom-call | flops 5368709120 | bytes 10485760 | tf_op jit(solution)/shard_map/pallas_call | solution.py:603
  252.5 0.1 constant_dynamic-slice_fusion
  252.6 0.9 collective-permute-start
  253.5 2.4 collective-permute-done
  255.9 2.6 %add_convert_fusion = bf16[512,1024]{1,0:T(8,128)(2,1)} fusion(bf16[512,1024]{1,0:T(8,128)(2,1)} %collective-permute-done, bf16[1024,1024]{1,0:T(8,128)(2,1)S(1)} %shard_map.113, s32[]{:T(128)S(6)} %select_n.6), kind=kLoop, calls=%fused_computation | loop fusion | flops 2097152 | bytes 3145732 | tf_op jit(solution)/shard_map/convert_element_type | solution.py:707
Async XLA Ops:
  3.8 225.7 %copy-start = (s32[1024]{0:T(1024)S(1)}, s32[1024]{0:T(1024)}, u32[]{:S(2)}) copy-start(s32[1024]{0:T(1024)} %by_byte.1) | copy-start | bytes 12292
  229.8 1.2 copy-start.1
  231.0 1.2 copy-start.2
  252.6 3.3 %collective-permute-start = (bf16[512,1024]{1,0:T(8,128)(2,1)S(1)}, bf16[512,1024]{1,0:T(8,128)(2,1)}, u32[]{:S(2)}, u32[]{:S(2)}) collective-permute-start(bf16[512,1024]{1,0:T(8,128)(2,1)S(1)} %constant_dynamic-slice_fusion), channel_id=1, source_target_pairs={{0,1},{1,0},{2,3},{3,2},{4,5},{5,4},{6,7},{7,6},{8,9},{9,8},{10,11... | collective-permute-start | bytes 3145736 | tf_op jit(solution)/shard_map/ppermute | solution.py:36

commit v4 on v3

--- a/solution.py
+++ b/solution.py
@@ -50,12 +50,14 @@
 
 def block_kernel(
     patch, mlp_gain, up, down, kv_gain, kv_weight, byte_states, query_weight, count,
-    kv_out, query_out, count_out,
+    byte_patch, out_weight,
+    out,
+    kv_out, query_out, count_out, num, den, term_send, term_kept, term_got,
     up_all, down_all, tokens, hidden, core_send, core_got, kept, plane_send, plane_got, mixed,
     swap_send, swap_recv, chunk_recv, right_send, left_send,
     token_send, token_recv, half_send, half_recv,
     core_sems, plane_sems, plane_recv, mixed_send, mixed_recv, local_sems,
-    halo_send, halo_recv, count_send, count_recv,
+    halo_send, halo_recv, count_send, count_recv, term_sems, term_recv,
 ):
     seq, core = lax.axis_index("seq"), lax.axis_index("mp")
     depth = lax.axis_size("seq") // PLANE
@@ -216,6 +218,8 @@
                 count_over(turn).start()
 
     count_out[0] = count[...]
+    num[...] = jnp.zeros_like(num)
+    den[...] = jnp.zeros_like(den)
 
     @pl.when(z < depth - 1)
     def _():
@@ -333,6 +337,16 @@
         hidden[pl.ds(low, tall), :] = gelu.astype(jnp.bfloat16)
         hop(1, step)
 
+    for turn in range(1, PLANE):
+        send_tokens(turn).wait_send()
+        half_over(turn).wait_send()
+    kv_held = tokens.at[:, 0:half]
+    out_held = tokens.at[0 : out_weight.shape[0], half : 2 * half]
+    kv_load = pltpu.make_async_copy(kv_weight, kv_held, local_sems.at[0])
+    out_load = pltpu.make_async_copy(out_weight, out_held, local_sems.at[1])
+    kv_load.start()
+    out_load.start()
+
     near = jnp.minimum(z, depth - 1 - z)
 
     def order(turn):
@@ -342,7 +356,7 @@
     def plane_out(turn, to):
         start = pl.multiple_of(member(to) * rows, rows)
         return remote(
-            plane_send.at[turn, pl.ds(start, rows), :], plane_got.at[turn, to],
+            plane_send.at[turn, pl.ds(start, rows), :], plane_got.at[turn, to - 1],
             plane_sems.at[turn, to], plane_recv.at[turn, to], peer(to),
         )
 
@@ -398,7 +412,7 @@
         total = plane_send[turn, pl.ds(row_start, rows), :].astype(jnp.float32)
         for to in range(1, PLANE):
             plane_out(turn, to).wait_recv()
-            total = total + plane_got[turn, to].astype(jnp.float32)
+            total = total + plane_got[turn, to - 1].astype(jnp.float32)
         mixed[2 * order(turn) + core] = total.astype(jnp.bfloat16)
         mixed_over(turn, core).start()
 
@@ -406,6 +420,8 @@
     def _(turn):
         mixed_over(turn, 1 - core).wait_recv()
 
+    kv_load.wait()
+    out_load.wait()
     later_gain = kv_gain[...].astype(jnp.float32)
 
     @pl.loop(0, rows // TILE)
@@ -416,7 +432,7 @@
         )
         values = patch[pl.ds(low, TILE), :].astype(jnp.float32) + more.astype(jnp.float32)
         kv_in = scale_rows(values, later_gain).astype(jnp.bfloat16)
-        projected = jnp.dot(kv_in, kv_weight[...], preferred_element_type=jnp.float32)
+        projected = jnp.dot(kv_in, kv_held[...], preferred_element_type=jnp.float32)
         for head in range(heads):
             key = slice(head * 2 * HS, head * 2 * HS + HS)
             value = slice(head * 2 * HS + HS, (head + 1) * 2 * HS)
@@ -427,30 +443,129 @@
         def _():
             halo_on(tile).start()
 
-        for turn in range(1, PLANE):
+        for turn in range(1, PLANE - 1):
             @pl.when(later(turn))
             def _(turn=turn):
                 halo_over(turn, tile).start()
 
-    @pl.when(z > 0)
+    @pl.when(later(PLANE - 1))
     def _():
         @pl.loop(0, rows // TILE)
         def _(step):
+            halo_over(PLANE - 1, step).start()
+
+    scale = 2.0 / math.sqrt(HS) * math.log2(math.e)
+    byte_rows = byte_patch.shape[0] // PLANE
+
+    def attend_tile(slot, tile):
+        low = pl.multiple_of(tile * byte_rows, byte_rows)
+        here = pl.ds(low, byte_rows)
+        live = count_out[slot][0:1, 0:1]
+        before = jnp.zeros((1, 1), jnp.int32)
+        for back in range(1, PLANE + 1):
+            before = before + jnp.where(slot >= back, count_out[back][0:1, 0:1], 0)
+        mine = byte_patch[here, :] + before
+        for start in range(0, rows, KEY_TILE):
+            position = start + lax.broadcasted_iota(jnp.int32, (byte_rows, KEY_TILE), 1)
+            gap = mine - position
+            usable = (position < live) & (gap >= 0) & (gap < WIN)
+            keys = slice(start, start + KEY_TILE)
+            scores = [
+                lax.dot_general(
+                    query_out[here, head * HS : (head + 1) * HS],
+                    kv_out[slot, keys, head * 2 * HS : head * 2 * HS + HS],
+                    (((1,), (1,)), ((), ())),
+                    preferred_element_type=jnp.float32,
+                )
+                for head in range(heads)
+            ]
+            weights = [jnp.where(usable, jnp.exp2(score * scale), 0.0) for score in scores]
+            for head in range(heads):
+                columns = slice(head * HS, (head + 1) * HS)
+                weight = weights[head]
+                den[here, columns] += weight[:, :HS] + weight[:, HS:]
+                num[here, columns] += jnp.dot(
+                    weight.astype(jnp.bfloat16),
+                    kv_out[slot, keys, head * 2 * HS + HS : (head + 1) * 2 * HS],
+                    preferred_element_type=jnp.float32,
+                )
+
+    @pl.loop(0, PLANE)
+    def _(step):
+        @pl.when(z > 0)
+        def _():
             halo_on(step).wait_recv()
-            for turn in range(1, PLANE):
+            for turn in range(1, PLANE - 1):
                 @pl.when(member(turn) < place)
                 def _(turn=turn):
                     halo_over(turn, step).start()
 
+        attend_tile(0, step)
+
+    @pl.when((z > 0) & (member(PLANE - 1) < place))
+    def _():
+        @pl.loop(0, rows // TILE)
+        def _(step):
+            halo_over(PLANE - 1, step).start()
+
     for turn in range(1, PLANE):
         @pl.when((member(turn) < place) | (z > 0))
         def _(turn=turn):
             count_arrives(turn).wait_recv()
 
+    @pl.when(z > 0)
+    def _():
+        @pl.loop(0, PLANE)
+        def _(tile):
+            attend_tile(PLANE, tile)
+
+    @pl.loop(1, PLANE)
+    def _(turn):
+        @pl.when((member(turn) < place) | (z > 0))
+        def _():
             @pl.loop(0, rows // TILE)
             def _(step):
                 halo_arrives(turn, step).wait_recv()
 
+            @pl.loop(0, PLANE)
+            def _(tile):
+                attend_tile(from_distance(turn), tile)
+
+    def finish(tile):
+        low = pl.multiple_of(tile * byte_rows, byte_rows)
+        parts = []
+        for head in range(heads):
+            columns = slice(head * HS, (head + 1) * HS)
+            total = jnp.sum(den[pl.ds(low, byte_rows), columns], axis=1, keepdims=True)
+            parts.append((num[pl.ds(low, byte_rows), columns] / total).astype(jnp.bfloat16))
+        return jnp.dot(
+            jnp.concatenate(parts, axis=1), out_held[...], preferred_element_type=jnp.float32
+        ).astype(jnp.bfloat16)
+
+    pair = PLANE // 2
+
+    def term_over(tile):
+        return remote(
+            term_send.at[tile], term_got.at[tile], term_sems.at[tile], term_recv.at[tile], partner
+        )
+
+    @pl.loop(0, pair)
+    def _(tile):
+        term_send[tile] = finish((1 - core) * pair + tile)
+        term_over(tile).start()
+
+    @pl.loop(0, pair)
+    def _(tile):
+        term_kept[tile] = finish(core * pair + tile)
+
+    @pl.loop(0, pair)
+    def _(tile):
+        term_over(tile).wait()
+        total = term_kept[tile].astype(jnp.float32) + term_got[tile].astype(jnp.float32)
+        out[pl.ds(pl.multiple_of(tile * byte_rows, byte_rows), byte_rows), :] = total.astype(
+            jnp.bfloat16
+        )
+
     for turn in range(1, PLANE):
         @pl.when(later(turn) | (z > 0))
         def _(turn=turn):
@@ -471,8 +586,6 @@
     for turn in range(1, PLANE):
         for kind in range(2):
             swap(kind, turn).wait_send()
-        send_tokens(turn).wait_send()
-        half_over(turn).wait_send()
 
     @pl.loop(0, depth)
     def _(turn):
@@ -494,25 +607,32 @@
 
 
 def patch_block(
-    patch, mlp_gain, up, down, kv_gain, kv_weight, byte_states, query_weight, count, depth
+    patch, mlp_gain, up, down, kv_gain, kv_weight, byte_states, query_weight, count,
+    byte_patch, out_weight, depth
 ):
     rows, features = patch.shape
     thin = up.shape[0]
     units = up.shape[1] // PLANE
     wide = features // (2 * depth)
+    bytes_here, width = byte_states.shape[0], out_weight.shape[1]
     vmem = pl.BlockSpec(memory_space=pltpu.VMEM)
+    hbm = pl.BlockSpec(memory_space=pl.ANY)
     bf16 = lambda *shape: pltpu.VMEM(shape, jnp.bfloat16)
     dma = lambda *shape: pltpu.SemaphoreType.DMA(shape)
     return pl.pallas_call(
         block_kernel,
-        in_specs=[vmem] * 9,
-        out_specs=[vmem] * 3,
-        out_shape=[
-            jax.ShapeDtypeStruct((PLANE + 1, rows, kv_weight.shape[1]), jnp.bfloat16),
-            jax.ShapeDtypeStruct((byte_states.shape[0], query_weight.shape[1]), jnp.bfloat16),
-            jax.ShapeDtypeStruct((PLANE + 1, 8, 128), jnp.int32),
-        ],
+        in_specs=[vmem] * 5 + [hbm] + [vmem] * 4 + [hbm],
+        out_specs=vmem,
+        out_shape=jax.ShapeDtypeStruct((bytes_here // 2, width), jnp.bfloat16),
         scratch_shapes=[
+            bf16(PLANE + 1, rows, kv_weight.shape[1]),
+            bf16(bytes_here, query_weight.shape[1]),
+            pltpu.VMEM((PLANE + 1, 8, 128), jnp.int32),
+            pltpu.VMEM((bytes_here, query_weight.shape[1]), jnp.float32),
+            pltpu.VMEM((bytes_here, query_weight.shape[1]), jnp.float32),
+            bf16(2, bytes_here // 4, width),
+            bf16(2, bytes_here // 4, width),
+            bf16(2, bytes_here // 4, width),
             bf16(features, units),
             bf16(depth * PLANE, units, thin),
             bf16(PLANE * rows, features),
@@ -521,23 +641,24 @@
             bf16(depth, PLANE * rows, wide),
             bf16(PLANE * rows, wide),
             bf16(depth, PLANE * rows, wide),
-            bf16(depth, PLANE, rows, wide),
+            bf16(depth, PLANE - 1, rows, wide),
             bf16(2 * depth, rows, wide),
             dma(2, PLANE), dma(2, PLANE), dma(2, depth * PLANE),
             dma(2, depth * PLANE), dma(2, depth * PLANE),
             dma(PLANE), dma(PLANE), dma(PLANE), dma(PLANE),
             dma(2, depth), dma(depth, PLANE), dma(depth, PLANE), dma(depth), dma(depth), dma(2),
             dma(PLANE, rows // TILE), dma(PLANE, rows // TILE), dma(PLANE), dma(PLANE),
+            dma(2), dma(2),
         ],
         compiler_params=pltpu.CompilerParams(
-            collective_id=0, has_side_effects=True, vmem_limit_bytes=62 * 2**20
+            collective_id=0, has_side_effects=True, vmem_limit_bytes=60 * 2**20
         ),
         cost_estimate=pl.CostEstimate(
             flops=40 * 10**9, bytes_accessed=60 * 10**6, transcendentals=0
         ),
     )(
         patch, mlp_gain[None], up, down, kv_gain[None], kv_weight, byte_states, query_weight,
-        jnp.broadcast_to(count, (8, 128)),
+        jnp.broadcast_to(count, (8, 128)), byte_patch[:, None], out_weight,
     )
 
 
@@ -691,17 +812,17 @@
     depth = (WIN + fewest - 2) // fewest
     fits = seq == 4 * PLANE and lax.axis_size("mp") == 2 and depth == PLANE
     fits = fits and up_weight.shape[0] % 128 == 0 and up_weight.shape[1] % (PLANE * 128) == 0
+    fits = fits and PLANE * patch_rows == patch_states.shape[1] == 2 * kv_weight.shape[1]
+    fits = fits and out_weight.shape[1] == kv_weight.shape[1]
     if fits:
-        kv_all, queries, counts = patch_block(*operands, patch_counts, seq // PLANE)
-        counts = counts[:, 0, 0]
-    else:
-        kv_pack, queries = patch_block_plain(*operands)
-        kv_all, counts = [kv_pack], [patch_counts]
-        for back in range(1, depth + 1):
-            pairs = [(i, i + back) for i in range(max(0, seq - back))]
-            kv_all.append(lax.ppermute(kv_pack, "seq", pairs))
-            counts.append(lax.ppermute(patch_counts, "seq", pairs))
-        kv_all, counts = jnp.stack(kv_all), jnp.concatenate(counts)
+        return patch_block(*operands, patch_counts, byte_patch, out_weight, seq // PLANE)
+    kv_pack, queries = patch_block_plain(*operands)
+    kv_all, counts = [kv_pack], [patch_counts]
+    for back in range(1, depth + 1):
+        pairs = [(i, i + back) for i in range(max(0, seq - back))]
+        kv_all.append(lax.ppermute(kv_pack, "seq", pairs))
+        counts.append(lax.ppermute(patch_counts, "seq", pairs))
+    kv_all, counts = jnp.stack(kv_all), jnp.concatenate(counts)
     kv_all = kv_all.reshape((depth + 1) * patch_rows, kv_all.shape[2])
     term = attend(queries, byte_patch, counts, kv_all, out_weight)
     return sum_over_cores(term, 0).astype(jnp.bfloat16)

time: 260 us -> 241 us (0.927)
  Pallas kernels: 245 us -> 230 us
    pallas_call x2 -> x1, Pallas kernels: 245 us -> 230 us  [patch_block(): pl.pallas_call(block_kernel, in_specs=[vmem] * 5 + [hbm] + [vmem] * 4 + [...]
  transfers between devices with their start and end apart: 1 -> 0, of which waited for: 1 -> 0; matrix products, arithmetic and copies ran while one was open for 0% -> 0% of each run, Pallas kernels for 0% -> 0%
where the time goes in v4:
time: 241 us; the launch traced here: 237 us
  Pallas kernels  230 us (95%)
  local copies, waits for them, and re-layouts  7.13 us (3%)
    pallas_call x1, Pallas kernels, patch_block(): pl.pallas_call(block_kernel, in_specs=[vmem] * 5 + [hbm] + [vmem] * 4 + [...  230 us

profile of v4, /device:TPU:9, one launch (start us, length us, event | category | flops | bytes accessed | tf_op | source)
XLA Modules:
  0.0 237.4 jit_solution(6323511246851701684)
XLA Ops:
  0.7 0.6 broadcast_in_dim.16.count
  1.2 1.3 broadcast_in_dim.14.mlp_gain
  2.5 1.3 broadcast_in_dim.15.kv_gain
  3.8 1.7 copy.12.byte_patch
  5.5 229.6 %shard_map.112 = bf16[512,1024]{1,0:T(8,128)(2,1)} custom-call(bf16[512,2048]{1,0:T(8,128)(2,1)} %patch.1, bf16[1,2048]{1,0:T(2,128)(2,1)} %broadcast_in_dim.14.mlp_gain, bf16[128,3584]{1,0:T(8,128)(2,1)} %up.1, bf16[3584,128]{1,0:T(8,128)(2,1)} %down.1, bf16[1,2048]{1,0:T(2,128)(2,1)} %broadcast_in_dim.15.kv_gain, bf16[2048,1024]{1,0:T(8,128)(2,1)} %kv_weight.1, ...), custom_call_target="tpu_custom_call" | custom-call | flops 40000000000 | bytes 60000000 | tf_op jit(solution)/shard_map/pallas_call | solution.py:622
  235.1 2.3 copy.15

commit v5 on v4

--- a/solution.py
+++ b/solution.py
@@ -48,11 +48,15 @@
     return jnp.concatenate([first, second], axis=dim)
 
 
+def one_row(folded):
+    return jnp.concatenate([folded[i : i + 1, :] for i in range(folded.shape[0])], axis=1)
+
+
 def block_kernel(
     patch, mlp_gain, up, down, kv_gain, kv_weight, byte_states, query_weight, count,
-    byte_patch, out_weight,
+    byte_patch_rows, out_weight,
     out,
-    kv_out, query_out, count_out, num, den, term_send, term_kept, term_got,
+    kv_out, query_out, count_out, num, den, term_send, term_kept, term_got, byte_patch,
     up_all, down_all, tokens, hidden, core_send, core_got, kept, plane_send, plane_got, mixed,
     swap_send, swap_recv, chunk_recv, right_send, left_send,
     token_send, token_recv, half_send, half_recv,
@@ -176,8 +180,9 @@
         own[kind].start()
     for turn in range(1, PLANE):
         swap(0, turn).start()
-    own[0].wait()
-    spread(0, seq)
+    for kind in range(2):
+        own[kind].wait()
+        spread(kind, seq)
 
     def later(turn):
         return member(turn) > place
@@ -220,6 +225,9 @@
     count_out[0] = count[...]
     num[...] = jnp.zeros_like(num)
     den[...] = jnp.zeros_like(den)
+    turned = jnp.transpose(byte_patch_rows[...])
+    for i in range(byte_patch_rows.shape[0]):
+        byte_patch[i * 128 : (i + 1) * 128, :] = turned[:, i : i + 1]
 
     @pl.when(z < depth - 1)
     def _():
@@ -244,7 +252,7 @@
         part = kv_out.at[from_distance(turn), piece(step), :]
         return remote(part, part, halo_send.at[turn, step], halo_recv.at[turn, step], peer(turn))
 
-    gain = mlp_gain[...].astype(jnp.float32)
+    gain = one_row(mlp_gain[...].astype(jnp.float32))
     row_start = pl.multiple_of(place * rows, rows)
 
     @pl.loop(0, rows // TILE)
@@ -304,8 +312,6 @@
         hop(0, step)
 
     count_chain()
-    own[1].wait()
-    spread(1, seq)
     for turn in range(1, PLANE):
         swap_arrives(1, turn).wait_recv()
         spread(1, z * PLANE + member(turn))
@@ -422,7 +428,7 @@
 
     kv_load.wait()
     out_load.wait()
-    later_gain = kv_gain[...].astype(jnp.float32)
+    later_gain = one_row(kv_gain[...].astype(jnp.float32))
 
     @pl.loop(0, rows // TILE)
     def _(tile):
@@ -633,6 +639,7 @@
             bf16(2, bytes_here // 4, width),
             bf16(2, bytes_here // 4, width),
             bf16(2, bytes_here // 4, width),
+            pltpu.VMEM((bytes_here, 1), jnp.int32),
             bf16(features, units),
             bf16(depth * PLANE, units, thin),
             bf16(PLANE * rows, features),
@@ -657,8 +664,8 @@
             flops=40 * 10**9, bytes_accessed=60 * 10**6, transcendentals=0
         ),
     )(
-        patch, mlp_gain[None], up, down, kv_gain[None], kv_weight, byte_states, query_weight,
-        jnp.broadcast_to(count, (8, 128)), byte_patch[:, None], out_weight,
+        patch, mlp_gain.reshape(-1, 128), up, down, kv_gain.reshape(-1, 128), kv_weight, byte_states, query_weight,
+        jnp.broadcast_to(count, (8, 128)), byte_patch.reshape(-1, 128), out_weight,
     )
 
 
@@ -813,7 +820,7 @@
     fits = seq == 4 * PLANE and lax.axis_size("mp") == 2 and depth == PLANE
     fits = fits and up_weight.shape[0] % 128 == 0 and up_weight.shape[1] % (PLANE * 128) == 0
     fits = fits and PLANE * patch_rows == patch_states.shape[1] == 2 * kv_weight.shape[1]
-    fits = fits and out_weight.shape[1] == kv_weight.shape[1]
+    fits = fits and out_weight.shape[1] == kv_weight.shape[1] and byte_patch.shape[0] == 1024
     if fits:
         return patch_block(*operands, patch_counts, byte_patch, out_weight, seq // PLANE)
     kv_pack, queries = patch_block_plain(*operands)

time: 241 us -> 234 us (0.971)
  local copies, waits for them, and re-layouts: 7.13 us -> 2.86 us
  Pallas kernels: 230 us -> 227 us
    broadcast_in_dim x3 -> x0, local copies, waits for them, and re-layouts: 4.28 us -> none  [the longest x1 1.71 us: patch_block(): byte_patch[:, None]]
where the time goes in v5:
time: 234 us; the launch traced here: 231 us
  Pallas kernels  227 us (97%)
  local copies, waits for them, and re-layouts  2.86 us (1%)
    pallas_call x1, Pallas kernels, patch_block(): pl.pallas_call(block_kernel, in_specs=[vmem] * 5 + [hbm] + [vmem] * 4 + [...  227 us

profile of v5, /device:TPU:9, one launch (start us, length us, event | category | flops | bytes accessed | tf_op | source)
XLA Modules:
  0.0 230.8 jit_solution(15132376686891600354)
XLA Ops:
  0.7 0.6 broadcast_in_dim.2.count
  1.2 227.3 %shard_map.112 = bf16[512,1024]{1,0:T(8,128)(2,1)} custom-call(bf16[512,2048]{1,0:T(8,128)(2,1)} %patch.1, bf16[16,128]{1,0:T(8,128)(2,1)} %bitcast.5, bf16[128,3584]{1,0:T(8,128)(2,1)} %up.1, bf16[3584,128]{1,0:T(8,128)(2,1)} %down.1, bf16[16,128]{1,0:T(8,128)(2,1)} %bitcast.6, bf16[2048,1024]{1,0:T(8,128)(2,1)} %kv_weight.1, ...), custom_call_target="tpu_custom_call" | custom-call | flops 40000000000 | bytes 60000000 | tf_op jit(solution)/shard_map/pallas_call | solution.py:628
  228.5 2.3 copy.14
